TPU v7x, 32 devices: a whole 2x2x4 slice. The times are simulated.
32 devices in a mesh: groups: 2 (over x), space: 16 (over z, y, core).
Axes of the slice: x: 2, y: 2, z: 4, core: 2. Of those that a mesh axis runs over, the one named last changes fastest.
Arguments:
- slide_map: float32 [256, 416, 128], P(('groups', 'space')), parts along dimension 0
- kernels: float32 [8, 3, 3, 416], replicated, may hold values from -2 to 2
- pointwise: float32 [8, 416, 416], replicated, may hold values from -0.3125 to 0.3125
- biases: float32 [8, 416], replicated, may hold values from -3 to 3
- classifier: float32 [416, 2], replicated, may hold values from -0.3125 to 0.3125
Outputs:
- features: float32 [256, 416, 128], P(('groups', 'space')), parts along dimension 0
- logits: float32 [4], P('groups'), parts along dimension 0
There are 2 independent parts, one for each index of `groups`. A program takes and returns all parts, laid end to end along the dimension named above; an argument that names none is the same for every part. Nothing has to cross between parts.
All inputs are finite; a program needn't handle non-finite values.
Results may differ from a plain program's by a relative error of at most 0.00021.
Values sent between devices are 32-bit elements; how exact they have to be, the bound alone decides.
No kernel may reach another device: no remote copies, remote signals or barrier semaphores. Data moves between devices by JAX's collectives and lax.ppermute only.
A program may use at most 64 MiB of HBM per device.

v0:
```python
import functools

import jax
import jax.numpy as jnp
import numpy as np
from jax import lax
from jax.experimental import pallas as pl
from jax.experimental.pallas import tpu as pltpu
from jax.sharding import PartitionSpec as P

F32, BF16 = jnp.float32, jnp.bfloat16
LANES = 128
CHUNK = 16
STAGE = 4
VMEM_LIMIT = 56 * 2**20
HBM = pl.BlockSpec(memory_space=pl.ANY)
VMEM = pl.BlockSpec(memory_space=pltpu.VMEM)


class Plan:
    def __init__(self, own, channels, count):
        self.own, self.channels, self.count = own, channels, count
        self.body = channels // LANES * LANES
        self.tail = channels - self.body
        self.tail_at = 3 * self.body
        self.bias_lane = 3 * self.tail
        self.depth = self.tail_at + LANES

    def offsets(self, start):
        if start < self.body:
            return start, self.body + start, 2 * self.body + start
        at = self.tail_at + start - self.body
        return at, at + self.tail, at + 2 * self.tail

    def position(self):
        position = lax.axis_index("space")
        odd = lax.rem(position, 2) == 1
        has_next = jnp.logical_and(position > 0, position < self.count - 1)
        return odd, has_next


def fill_ones(plan, stacked):
    rows = LANES - plan.bias_lane
    index = lax.broadcasted_iota(jnp.int32, (rows, stacked.shape[1]), 0)
    stacked[plan.tail_at + plan.bias_lane :, :] = jnp.where(index < 3, 1.0, 0.0).astype(BF16)


def depthwise(plan, load, taps, stacked, column):
    for start in range(0, plan.channels, CHUNK):
        part = pl.ds(start, CHUNK)
        tap = [taps[part, LANES * j : LANES * (j + 1)] for j in range(9)]
        rows = [jnp.maximum(load(k, part), 0.0) for k in range(4)]
        at = plan.offsets(start)
        for r in range(2):
            left, mid, right = (
                tap[b] * rows[r] + tap[3 + b] * rows[r + 1] + tap[6 + b] * rows[r + 2]
                for b in range(3)
            )
            total = pltpu.roll(left, 1, 1) + mid + pltpu.roll(right, LANES - 1, 1)
            high = total.astype(BF16)
            low = (total - high.astype(F32)).astype(BF16)
            place = pl.ds(column + LANES * r, LANES)
            stacked[pl.ds(at[0], CHUNK), place] = high
            stacked[pl.ds(at[1], CHUNK), place] = high
            stacked[pl.ds(at[2], CHUNK), place] = low


def make_taps(kern, spread, taps):
    high = kern.astype(BF16)
    rest = kern - high.astype(F32)
    mid = rest.astype(BF16)
    low = (rest - mid.astype(F32)).astype(BF16)
    parts = jnp.concatenate([high, mid, low], axis=0)
    taps[...] = lax.dot_general(
        parts, spread, (((0,), (0,)), ((), ())), preferred_element_type=F32
    )


def make_mix(plan, weight, taps, mix):
    body = plan.body
    main = weight[:, :body]
    high = main.astype(BF16)
    mix[:, :body] = high
    mix[:, body : 2 * body] = (main - high.astype(F32)).astype(BF16)
    mix[:, 2 * body : 3 * body] = high
    last = weight[:, body:]
    top = last.astype(BF16).astype(F32)
    rest = jnp.zeros((plan.channels, LANES - 3 * plan.tail), F32)
    tile = jnp.concatenate([top, last - top, top, rest], axis=1)
    mix[:, plan.tail_at :] = (tile + taps[:, 9 * LANES :]).astype(BF16)


def run_level(plan, pairs, load, old, taps, mix, stacked, store, between=None):
    for p in range(pairs):
        depthwise(plan, lambda k, part, p=p: load(2 * p + k, part), taps, stacked, 256 * p)
    if between is not None:
        between()
    for p in range(pairs):
        mixed = jnp.dot(mix[...], stacked[:, 256 * p : 256 * (p + 1)], preferred_element_type=F32)
        for r in range(2):
            k = 2 * p + r
            store(k, old(k) + mixed[:, LANES * r : LANES * (r + 1)])


def edges_kernel(plan, source, near, far, sems):
    odd, _ = plan.position()
    half = source.shape[0] - STAGE
    far_at = jnp.where(odd, half, 0)
    copies = [
        pltpu.make_async_copy(source.at[pl.ds(half - far_at, STAGE)], near, sems.at[0]),
        pltpu.make_async_copy(source.at[pl.ds(far_at, STAGE)], far, sems.at[1]),
    ]
    for copy in copies:
        copy.start()
    for copy in copies:
        copy.wait()


def edges(plan, source):
    shape = jax.ShapeDtypeStruct((STAGE,) + source.shape[1:], F32)
    return pl.pallas_call(
        functools.partial(edges_kernel, plan),
        out_shape=[shape, shape],
        in_specs=[HBM],
        out_specs=[HBM, HBM],
        scratch_shapes=[pltpu.SemaphoreType.DMA((2,))],
    )(source)


def add_rows(sums, rows):
    total = rows[0]
    for row in rows[1:]:
        total = total + row
    sums[...] = total


def trapezoid_kernel(plan, start, *refs):
    first = start == 0
    own, side = plan.own, STAGE
    refs = list(refs)
    inputs = [refs.pop(0) for _ in range(2 if first else 4)]
    weights, kern, spread = refs.pop(0), refs.pop(0), refs.pop(0)
    mixes = refs.pop(0)
    behind = [refs.pop(0) for _ in range(STAGE)]
    final = refs.pop(0)
    sums = None if first else refs.pop(0)
    rows = [refs.pop(0) for _ in range(STAGE + 1)]
    weight, mix, taps, stacked, sem_rows, sem_w, sem_out = refs
    odd, _ = plan.position()

    arrive = []
    for l in range(STAGE):
        copy = pltpu.make_async_copy(weights.at[start + l], weight.at[l], sem_w.at[l])
        if l == 0:
            copy.start()
        arrive.append(copy)
    pieces = []
    if first:
        near, mine = inputs
        for k in range(side):
            pieces.append((near.at[k], jnp.where(odd, k, side - 1 - k)))
        for k in range(own):
            pieces.append((mine.at[k], side + jnp.where(odd, k, own - 1 - k)))
    else:
        near, low, mid, high = inputs
        for k in range(side):
            pieces.append((near.at[k], side - 1 - k))
        at = side
        for piece in (low, mid, high):
            for k in range(piece.shape[0]):
                pieces.append((piece.at[k], at))
                at += 1
    moves = [pltpu.make_async_copy(s, rows[0].at[d], sem_rows.at[i]) for i, (s, d) in enumerate(pieces)]
    for move in moves:
        move.start()
    for copy in arrive[1:]:
        copy.start()
    picked = spread[jnp.where(odd, 1, 0)]
    make_taps(kern[start], picked, taps.at[0])
    for s in range(2):
        fill_ones(plan, stacked.at[s])
    leave = []

    def send(index, source, target):
        copy = pltpu.make_async_copy(source, target, sem_out.at[index])
        copy.start()
        leave.append(copy)

    arrive[0].wait()
    make_mix(plan, weight.at[0], taps.at[0], mix.at[0])
    for move in moves:
        move.wait()
    for l in range(STAGE):
        source, target = rows[l], rows[l + 1]
        count = own + side - 2 * (l + 1)
        send(l, source.at[pl.ds(count, 2)], behind[l])
        send(STAGE + l, mix.at[l], mixes.at[l])

        def store(k, value, target=target):
            target[k] = value

        def between(l=l):
            if l + 1 < STAGE:
                make_taps(kern[start + l + 1], picked, taps.at[(l + 1) % 2])
                arrive[l + 1].wait()
                make_mix(plan, weight.at[l + 1], taps.at[(l + 1) % 2], mix.at[l + 1])

        run_level(
            plan, count // 2,
            lambda k, part, source=source: source[k, part, :],
            lambda k, source=source: source[k + 1],
            taps.at[l % 2], mix.at[l], stacked.at[l % 2], store, between,
        )
    last = rows[STAGE]
    if first:
        send(2 * STAGE, last, final)
    else:
        for k in range(side):
            send(2 * STAGE + k, last.at[k], final.at[jnp.where(odd, k, own - 1 - k)])
        add_rows(sums, [last[k] for k in range(side)])
    for copy in leave:
        copy.wait()


def trapezoid(plan, start, inputs, weights, kern, spread):
    channels, width = plan.channels, inputs[0].shape[-1]
    first = start == 0
    shape = lambda *s: jax.ShapeDtypeStruct(s, F32)
    outs = [jax.ShapeDtypeStruct((STAGE, channels, plan.depth), BF16)]
    outs += [shape(2, channels, width)] * STAGE
    outs += [shape(STAGE if first else plan.own, channels, width)]
    specs = [HBM] * len(outs)
    if not first:
        outs.append(shape(channels, width))
        specs.append(VMEM)
    reach = plan.own + STAGE
    return pl.pallas_call(
        functools.partial(trapezoid_kernel, plan, start),
        out_shape=outs,
        in_specs=[HBM] * (len(inputs) + 1) + [VMEM, VMEM],
        out_specs=specs,
        scratch_shapes=[pltpu.VMEM((reach - 2 * l, channels, width), F32) for l in range(STAGE + 1)]
        + [
            pltpu.VMEM((STAGE, channels, channels), F32),
            pltpu.VMEM((STAGE, channels, plan.depth), BF16),
            pltpu.VMEM((2, channels, 10 * LANES), F32),
            pltpu.VMEM((2, plan.depth, LANES * (reach - 2)), BF16),
            pltpu.SemaphoreType.DMA((reach,)),
            pltpu.SemaphoreType.DMA((STAGE,)),
            pltpu.SemaphoreType.DMA((3 * STAGE,)),
        ],
        compiler_params=pltpu.CompilerParams(vmem_limit_bytes=VMEM_LIMIT),
    )(*inputs, weights, kern, spread)


def wave_kernel(plan, start, stop, count, base, order, keep_from, ending, *refs):
    levels = stop - start
    refs = list(refs)
    fresh = refs.pop(0)
    behind_in = [refs.pop(0) for _ in range(levels)]
    mixes = [refs.pop(0) for _ in range(2)]
    kern, spread = refs.pop(0), refs.pop(0)
    if ending:
        refs.pop(0)
        sums_in = refs.pop(0)
    else:
        sums_in = None
    behind_out = {l: refs.pop(0) for l in range(max(start, keep_from), stop)}
    if ending:
        final, sums = refs.pop(0), refs.pop(0)
    else:
        ends = [refs.pop(0) for _ in range(count // 2)]
    rows = [refs.pop(0) for _ in range(levels + 1)]
    behind, mix, taps, stacked, sem_rows, sem_b, sem_w, sem_out = refs
    odd, has_next = plan.position()

    moves = []
    for k in range(count):
        if order == "mirror":
            place = jnp.where(odd, k, count - 1 - k)
        else:
            place = count - 1 - k
        moves.append(pltpu.make_async_copy(fresh.at[k], rows[0].at[place], sem_rows.at[k]))
    for move in moves:
        move.start()
    tails, weights = [], []
    for l in range(levels):
        tails.append(pltpu.make_async_copy(behind_in[l], behind.at[l], sem_b.at[l]))
        block = start + l
        weights.append(
            pltpu.make_async_copy(mixes[block // STAGE].at[block % STAGE], mix.at[l], sem_w.at[l])
        )
    for l in range(levels):
        tails[l].start()
        weights[l].start()
    picked = spread[jnp.where(odd, 1, 0)]
    make_taps(kern[start], picked, taps.at[0])
    for s in range(2):
        fill_ones(plan, stacked.at[s])
    for move in moves:
        move.wait()
    leave = []

    def send(index, source, target):
        copy = pltpu.make_async_copy(source, target, sem_out.at[index])
        copy.start()
        leave.append(copy)

    for l in range(levels):
        source, target = rows[l], rows[l + 1]
        if start + l in behind_out:
            send(l, source.at[pl.ds(count - 2, 2)], behind_out[start + l])
        tails[l].wait()

        def store(k, value, l=l, target=target):
            if base - (start + l + 1) + k >= plan.own:
                value = jnp.where(has_next, value, 0.0)
            target[k] = value

        def between(l=l):
            if l + 1 < levels:
                make_taps(kern[start + l + 1], picked, taps.at[(l + 1) % 2])
            weights[l].wait()


        run_level(
            plan, count // 2,
            lambda k, part, l=l, source=source: (
                behind[l, k, part, :] if k < 2 else source[k - 2, part, :]
            ),
            lambda k, l=l, source=source: behind[l, 1] if k == 0 else source[k - 1],
            taps.at[l % 2], mix.at[l], stacked.at[l % 2], store, between,
        )
    last = rows[levels]
    if ending:
        for k in range(count):
            u = base - stop + k
            send(levels + k, last.at[k], final.at[jnp.where(odd, u, plan.own - 1 - u)])
        add_rows(sums, [sums_in[...]] + [last[k] for k in range(count)])
    else:
        for p in range(count // 2):
            send(levels + p, last.at[pl.ds(2 * p, 2)], ends[p])
    for copy in leave:
        copy.wait()


def wave(plan, start, stop, base, order, keep_from, fresh, behind, mixes, kern, spread, ending=None):
    count, channels, width = fresh.shape
    levels = stop - start
    pair = jax.ShapeDtypeStruct((2, channels, width), F32)
    outs = [pair] * (stop - max(start, keep_from))
    operands = [fresh, *behind, *mixes, kern, spread]
    in_specs = [HBM] * (len(operands) - 2) + [VMEM, VMEM]
    specs = [HBM] * len(outs)
    aliases = {}
    if ending is not None:
        aliases = {len(operands): len(outs)}
        operands += list(ending)
        in_specs += [HBM, VMEM]
        outs += [jax.ShapeDtypeStruct(e.shape, F32) for e in ending]
        specs += [HBM, VMEM]
    else:
        outs += [pair] * (count // 2)
        specs += [HBM] * (count // 2)
    return pl.pallas_call(
        functools.partial(
            wave_kernel, plan, start, stop, count, base, order, keep_from, ending is not None
        ),
        out_shape=outs,
        in_specs=in_specs,
        out_specs=specs,
        scratch_shapes=[pltpu.VMEM(fresh.shape, F32)] * (levels + 1)
        + [
            pltpu.VMEM((levels, 2, channels, width), F32),
            pltpu.VMEM((levels, channels, plan.depth), BF16),
            pltpu.VMEM((2, channels, 10 * LANES), F32),
            pltpu.VMEM((2, plan.depth, LANES * count), BF16),
            pltpu.SemaphoreType.DMA((count,)),
            pltpu.SemaphoreType.DMA((levels,)),
            pltpu.SemaphoreType.DMA((levels,)),
            pltpu.SemaphoreType.DMA((levels + count,)),
        ],
        input_output_aliases=aliases,
        compiler_params=pltpu.CompilerParams(vmem_limit_bytes=VMEM_LIMIT),
    )(*operands)


def spread_matrix(plan):
    both = np.zeros((2, 3, 16, 10, LANES), np.float32)
    for odd in range(2):
        for part in range(3):
            for a in range(3):
                for b in range(3):
                    row = 3 * (a if odd else 2 - a) + b
                    line = both[odd, part, row, 3 * a + b]
                    line[:] = 1.0
                    if b == 0:
                        line[LANES - 1] = 0.0
                    if b == 2:
                        line[0] = 0.0
            both[odd, part, 9, 9, plan.bias_lane + part] = 1.0
    return jnp.asarray(both.reshape(2, 48, 10 * LANES), BF16)


def per_device(count, slide_map, kernels, pointwise, biases, classifier):
    own, channels, width = slide_map.shape
    levels = kernels.shape[0]
    plan = Plan(own, channels, count)
    near = [(i, i ^ 1) for i in range(count)]
    far = [(i, i + 1) for i in range(1, count - 1, 2)] + [(i + 1, i) for i in range(1, count - 1, 2)]
    send = lambda rows, pairs: lax.ppermute(rows, "space", pairs)

    near0, far0 = edges(plan, slide_map)
    near0, far0 = send(near0, near), send(far0, far)
    kern = jnp.concatenate([kernels.reshape(levels, 9, channels), biases[:, None]], axis=1)
    kern = jnp.pad(kern, ((0, 0), (0, 6), (0, 0)))
    spread = spread_matrix(plan)

    mix0, t0, t1, t2, t3, low4 = trapezoid(plan, 0, [near0, slide_map], pointwise, kern, spread)
    far2 = send(t2, far)
    near4 = send(low4, near)
    w2, w3, mid4, high4 = wave(
        plan, 0, 4, own, "mirror", 2, far0, [t0, t1, t2, t3], [mix0, mix0], kern, spread
    )
    far4 = send(mid4, far)
    mix4, t4, t5, t6, t7, features, sums = trapezoid(
        plan, 4, [near4, low4, mid4, high4], pointwise, kern, spread
    )
    mixes = [mix0, mix4]
    w4, w5, w6, w7, features, sums = wave(
        plan, 2, 8, own + 4, "reverse", 4, far2, [w2, w3, t4, t5, t6, t7], mixes, kern, spread,
        (features, sums),
    )
    features, sums = wave(
        plan, 4, 8, own + 6, "reverse", 8, far4, [w4, w5, w6, w7], mixes, kern, spread,
        (features, sums),
    )
    part = jnp.sum(jnp.sum(sums, axis=1)[:, None] * classifier, axis=0)
    part = part * (1.0 / (own * count * width))
    stride = 1
    while stride < count:
        part = part + send(part, [(i, i ^ stride) for i in range(count)])
        stride *= 2
    return features, part


def solution(mesh):
    in_specs = (P(("groups", "space"), None, None), P(), P(), P(), P())
    out_specs = (P(("groups", "space"), None, None), P("groups"))
    return jax.shard_map(
        functools.partial(per_device, mesh.shape["space"]),
        mesh=mesh, in_specs=in_specs, out_specs=out_specs, check_vma=False,
    )
```

profile of v0, /device:TPU:0, one launch (start us, length us, event | category | flops | bytes accessed | tf_op | source)
XLA Modules:
  0.0 149.1 jit_solution(13694084647870985981)
XLA Ops:
  0.6 52.7 %shard_map.77 = (f32[4,416,128]{2,1,0:T(8,128)}, f32[4,416,128]{2,1,0:T(8,128)}) custom-call(f32[8,416,128]{2,1,0:T(8,128)} %refs_1_.1), custom_call_target="tpu_custom_call" | custom-call | tf_op jit(solution)/shard_map/pallas_call | solution.py:121
  53.4 0.5 collective-permute-start.1
  53.9 0.7 collective-permute-start
  54.7 0.1 copy.11
  54.8 0.7 select_maximum_fusion.refs_3_.refs_7_.refs_5_.refs_9_
  55.5 0.6 collective-permute-done.1.refs_0_
  56.1 0.9 copy-done.2
  57.0 13.5 %shard_map.78 = (bf16[4,416,1280]{2,1,0:T(8,128)(2,1)}, f32[2,416,128]{2,1,0:T(8,128)}, f32[2,416,128]{2,1,0:T(8,128)}, f32[2,416,128]{2,1,0:T(8,128)}, f32[2,416,128]{2,1,0:T(8,128)}, /*index=5*/f32[4,416,128]{2,1,0:T(8,128)}) custom-call(f32[4,416,128]{2,1,0:T(8,128)} %copy-done.2, f32[8,416,128]{2,1,0:T(8,128)} %refs_1_.1, f32[8,416,416]{2,1,0:T(8,128)} %refs_4_.2, ...), custom_call_target="tpu_custom_call" | custom-call | tf_op jit(solution)/shard_map/pallas_call | solution.py:237
  70.6 3.3 %collective-permute-start.4 = (f32[4,416,128]{2,1,0:T(8,128)}, f32[4,416,128]{2,1,0:T(8,128)S(1)}, u32[]{:S(2)}, u32[]{:S(2)}) collective-permute-start(f32[4,416,128]{2,1,0:T(8,128)} %get-tuple-element.39.refs_1_), channel_id=1, source_target_pairs={{0,1},{1,0},{2,3},{3,2},{4,5},{5,4},{6,7},{7,6},{8,9},{9,8},{10,11... | collective-permute-start | bytes 2555912 | tf_op jit(solution)/shard_map/ppermute | solution.py:411
  73.9 0.9 collective-permute-start.3
  74.7 0.0 copy-start
  74.8 0.9 copy-done
  75.7 11.0 %shard_map.79 = (f32[2,416,128]{2,1,0:T(8,128)}, f32[2,416,128]{2,1,0:T(8,128)}, f32[2,416,128]{2,1,0:T(8,128)}, f32[2,416,128]{2,1,0:T(8,128)}) custom-call(f32[4,416,128]{2,1,0:T(8,128)} %copy-done, f32[2,416,128]{2,1,0:T(8,128)} %get-tuple-element.31.refs_1_, f32[2,416,128]{2,1,0:T(8,128)} %get-tuple-element.32.refs_2_, ...), custom_call_target="tpu_custom_call" | custom-call | tf_op jit(solution)/shard_map/pallas_call | solution.py:365
  86.6 0.7 collective-permute-start.2
  87.3 0.0 collective-permute-done.4.refs_0_
  87.3 0.9 copy-done.1
  88.2 14.1 %shard_map.80 = (bf16[4,416,1280]{2,1,0:T(8,128)(2,1)}, f32[2,416,128]{2,1,0:T(8,128)}, f32[2,416,128]{2,1,0:T(8,128)}, f32[2,416,128]{2,1,0:T(8,128)}, f32[2,41...) custom-call(f32[4,416,128]{2,1,0:T(8,128)} %copy-done.1, f32[4,416,128]{2,1,0:T(8,128)} %get-tuple-element.39.refs_1_, ...), custom_call_target="tpu_custom_call" | custom-call | tf_op jit(solution)/shard_map/pallas_call | solution.py:237
  102.3 0.8 copy-done.4
  103.1 14.6 %shard_map.81 = (f32[2,416,128]{2,1,0:T(8,128)}, f32[2,416,128]{2,1,0:T(8,128)}, f32[2,416,128]{2,1,0:T(8,128)}, f32[2,416,128]{2,1,0:T(8,128)}, f32[8,416,128]{2,1,0:T(8,128)}, /*index=5*/f32[416,128]{1,0:T(8,128)}) custom-call(f32[2,416,128]{2,1,0:T(8,128)} %copy-done.4, ...), custom_call_target="tpu_custom_call", output_to_operand_aliasing={{4}: (11, {})} | custom-call | tf_op jit(solution)/shard_map/pallas_call | solution.py:365
  117.7 0.8 copy-done.3
  118.5 10.1 %shard_map.82 = (f32[8,416,128]{2,1,0:T(8,128)}, f32[416,128]{1,0:T(8,128)}) custom-call(f32[2,416,128]{2,1,0:T(8,128)} %copy-done.3, f32[2,416,128]{2,1,0:T(8,128)} %get-tuple-element.48.refs_1_, f32[2,416,128]{2,1,0:T(8,128)} %get-tuple-element.49.refs_2_, f32[2,416,128]{2,1,0:T(8,128)} %get-tuple-element.50.refs_3_, ...), custom_call_target="tpu_custom_call", output_to_operand_aliasing={{0}: (9, {})} | custom-call | tf_op jit(solution)/shard_map/pallas_call | solution.py:365
  128.6 1.1 reduce_sum.18
  129.7 0.1 multiply_reduce_fusion
  129.8 6.4 %collective-permute-start.5 = (f32[2]{0:T(128)S(1)}, f32[2]{0:T(128)S(1)}, u32[]{:S(2)}, u32[]{:S(2)}) collective-permute-start(f32[2]{0:T(128)S(1)} %broadcast_multiply_fusion), channel_id=1, source_target_pairs={{0,1},{1,0},{2,3},{3,2},{4,5},{5,4},{6,7},{7,6},{8,9},{9,8},{10,11... | collective-permute-start | bytes 32 | tf_op jit(solution)/shard_map/ppermute | solution.py:411
  136.3 0.8 collective-permute-done.5
  137.1 0.3 collective-permute-start.6
  137.3 3.3 %collective-permute-done.6 = f32[2]{0:T(128)S(1)} collective-permute-done((f32[2]{0:T(128)S(1)}, f32[2]{0:T(128)S(1)}, u32[]{:S(2)}, u32[]{:S(2)}) %collective-permute-start.6) | collective-permute-done | bytes 40 | tf_op jit(solution)/shard_map/ppermute | solution.py:411
  140.6 1.6 %collective-permute-start.7 = (f32[2]{0:T(128)S(1)}, f32[2]{0:T(128)S(1)}, u32[]{:S(2)}, u32[]{:S(2)}) collective-permute-start(f32[2]{0:T(128)S(1)} %add.15), channel_id=1, source_target_pairs={{0,4},{1,5},{2,6},{3,7},{4,0},{5,1},{6,2},{7,3},{8,12},{9,13},{10,... | collective-permute-start | bytes 32 | tf_op jit(solution)/shard_map/ppermute | solution.py:411
  142.2 1.9 %collective-permute-done.7 = f32[2]{0:T(128)S(1)} collective-permute-done((f32[2]{0:T(128)S(1)}, f32[2]{0:T(128)S(1)}, u32[]{:S(2)}, u32[]{:S(2)}) %collective-permute-start.7) | collective-permute-done | bytes 40 | tf_op jit(solution)/shard_map/ppermute | solution.py:411
  144.2 2.6 %collective-permute-start.8 = (f32[2]{0:T(128)S(1)}, f32[2]{0:T(128)S(1)}, u32[]{:S(2)}, u32[]{:S(2)}) collective-permute-start(f32[2]{0:T(128)S(1)} %add.16), channel_id=1, source_target_pairs={{0,8},{1,9},{2,10},{3,11},{4,12},{5,13},{6,14},{7,15},{8,0},{9,1},... | collective-permute-start | bytes 32 | tf_op jit(solution)/shard_map/ppermute | solution.py:411
  146.8 1.8 %collective-permute-done.8 = f32[2]{0:T(128)S(1)} collective-permute-done((f32[2]{0:T(128)S(1)}, f32[2]{0:T(128)S(1)}, u32[]{:S(2)}, u32[]{:S(2)}) %collective-permute-start.8) | collective-permute-done | bytes 40 | tf_op jit(solution)/shard_map/ppermute | solution.py:411
  148.6 0.5 add.17
  (18 shorter events, 0.1 us)
Async XLA Ops:
  0.6 54.0 %copy-start.6 = (f32[8,416]{1,0:T(8,128)S(1)}, f32[8,416]{1,0:T(8,128)}, u32[]{:S(2)}) copy-start(f32[8,416]{1,0:T(8,128)} %param.9) | copy-start | bytes 39940
  0.6 54.0 %copy-start.5 = (f32[8,3,3,416]{3,0,2,1:T(8,128)S(1)}, f32[8,3,3,416]{3,0,2,1:T(8,128)}, u32[]{:S(2)}) copy-start(f32[8,3,3,416]{3,0,2,1:T(8,128)} %param.7) | copy-start | bytes 359428
  53.4 2.7 %collective-permute-start.1 = (f32[4,416,128]{2,1,0:T(8,128)}, f32[4,416,128]{2,1,0:T(8,128)S(1)}, u32[]{:S(2)}, u32[]{:S(2)}) collective-permute-start(f32[4,416,128]{2,1,0:T(8,128)} %get-tuple-element.30), channel_id=1, source_target_pairs={{0,1},{1,0},{2,3},{3,2},{4,5},{5,4},{6,7},{7,6},{8,9},{9,8},{10,11... | collective-permute-start | bytes 2555912 | tf_op jit(solution)/shard_map/ppermute | solution.py:411
  53.9 20.8 %collective-permute-start = (f32[4,416,128]{2,1,0:T(8,128)}, f32[4,416,128]{2,1,0:T(8,128)S(1)}, u32[]{:S(2)}, u32[]{:S(2)}) collective-permute-start(f32[4,416,128]{2,1,0:T(8,128)} %get-tuple-element.29), channel_id=1, source_target_pairs={{1,2},{3,4},{5,6},{7,8},{9,10},{11,12},{13,14},{2,1},{4,3},{6,5},{... | collective-permute-start | bytes 2555912 | tf_op jit(solution)/shard_map/ppermute | solution.py:411
  56.1 0.9 copy-start.2
  70.6 16.7 %collective-permute-start.4 = (f32[4,416,128]{2,1,0:T(8,128)}, f32[4,416,128]{2,1,0:T(8,128)S(1)}, u32[]{:S(2)}, u32[]{:S(2)}) collective-permute-start(f32[4,416,128]{2,1,0:T(8,128)} %get-tuple-element.39.refs_1_), channel_id=1, source_target_pairs={{0,1},{1,0},{2,3},{3,2},{4,5},{5,4},{6,7},{7,6},{8,9},{9,8},{10,11... | collective-permute-start | bytes 2555912 | tf_op jit(solution)/shard_map/ppermute | solution.py:411
  73.9 28.5 %collective-permute-start.3 = (f32[2,416,128]{2,1,0:T(8,128)}, f32[2,416,128]{2,1,0:T(8,128)S(1)}, u32[]{:S(2)}, u32[]{:S(2)}) collective-permute-start(f32[2,416,128]{2,1,0:T(8,128)} %get-tuple-element.33.refs_3_), channel_id=1, source_target_pairs={{1,2},{3,4},{5,6},{7,8},{9,10},{11,12},{13,14},{2,1},{4,3},{6,5},{... | collective-permute-start | bytes 1277960 | tf_op jit(solution)/shard_map/ppermute | solution.py:411
  74.7 0.9 copy-start
  86.6 31.1 %collective-permute-start.2 = (f32[2,416,128]{2,1,0:T(8,128)}, f32[2,416,128]{2,1,0:T(8,128)S(1)}, u32[]{:S(2)}, u32[]{:S(2)}) collective-permute-start(f32[2,416,128]{2,1,0:T(8,128)} %get-tuple-element.36.refs_2_), channel_id=1, source_target_pairs={{1,2},{3,4},{5,6},{7,8},{9,10},{11,12},{13,14},{2,1},{4,3},{6,5},{... | collective-permute-start | bytes 1277960 | tf_op jit(solution)/shard_map/ppermute | solution.py:411
  87.3 0.9 copy-start.1
  102.3 0.8 copy-start.4
  117.7 0.8 copy-start.3
  118.5 11.2 %copy-start.7 = (f32[416,2]{0,1:T(2,128)S(1)}, f32[416,2]{0,1:T(2,128)}, u32[]{:S(2)}) copy-start(f32[416,2]{0,1:T(2,128)} %param.10) | copy-start | bytes 9988
  129.8 7.3 %collective-permute-start.5 = (f32[2]{0:T(128)S(1)}, f32[2]{0:T(128)S(1)}, u32[]{:S(2)}, u32[]{:S(2)}) collective-permute-start(f32[2]{0:T(128)S(1)} %broadcast_multiply_fusion), channel_id=1, source_target_pairs={{0,1},{1,0},{2,3},{3,2},{4,5},{5,4},{6,7},{7,6},{8,9},{9,8},{10,11... | collective-permute-start | bytes 32 | tf_op jit(solution)/shard_map/ppermute | solution.py:411
  137.1 3.5 %collective-permute-start.6 = (f32[2]{0:T(128)S(1)}, f32[2]{0:T(128)S(1)}, u32[]{:S(2)}, u32[]{:S(2)}) collective-permute-start(f32[2]{0:T(128)S(1)} %fusion), channel_id=1, source_target_pairs={{0,2},{1,3},{2,0},{3,1},{4,6},{5,7},{6,4},{7,5},{8,10},{9,11},{10,... | collective-permute-start | bytes 32 | tf_op jit(solution)/shard_map/ppermute | solution.py:411
  140.6 3.5 %collective-permute-start.7 = (f32[2]{0:T(128)S(1)}, f32[2]{0:T(128)S(1)}, u32[]{:S(2)}, u32[]{:S(2)}) collective-permute-start(f32[2]{0:T(128)S(1)} %add.15), channel_id=1, source_target_pairs={{0,4},{1,5},{2,6},{3,7},{4,0},{5,1},{6,2},{7,3},{8,12},{9,13},{10,... | collective-permute-start | bytes 32 | tf_op jit(solution)/shard_map/ppermute | solution.py:411
  144.2 4.4 %collective-permute-start.8 = (f32[2]{0:T(128)S(1)}, f32[2]{0:T(128)S(1)}, u32[]{:S(2)}, u32[]{:S(2)}) collective-permute-start(f32[2]{0:T(128)S(1)} %add.16), channel_id=1, source_target_pairs={{0,8},{1,9},{2,10},{3,11},{4,12},{5,13},{6,14},{7,15},{8,0},{9,1},... | collective-permute-start | bytes 32 | tf_op jit(solution)/shard_map/ppermute | solution.py:411
where the time goes:
time: 149 us
  Pallas kernels  116 us (78%)
  starting transfers between devices  17 us (11%)
  waiting for transfers between devices  8.51 us (6%)
  local copies, waits for them, and re-layouts  4.34 us (3%)
  other arithmetic  2.47 us (2%)
    pallas_call x1, Pallas kernels, edges(): pl.pallas_call(functools.partial(edges_kernel, plan), out_shape=[shape, s...  52.7 us
    pallas_call x3, Pallas kernels, wave(): pl.pallas_call(functools.partial(wave_kernel, plan, start, stop, count, b...  35.6 us
    pallas_call x2, Pallas kernels, trapezoid(): pl.pallas_call(functools.partial(trapezoid_kernel, plan, start), out_shap...  27.6 us
    ppermute x9, starting transfers between devices, per_device(): send = lambda rows, pairs: lax.ppermute(rows, 'space', pairs)  17 us
    ppermute x9, waiting for transfers between devices, per_device(): send = lambda rows, pairs: lax.ppermute(rows, 'space', pairs)  8.51 us
    unnamed x16, local copies, waits for them, and re-layouts  4.23 us
  transfers between devices with their start and end apart: 9, of which 5 were waited for; matrix products, arithmetic and copies ran while one was open for 1% of the time, Pallas kernels for 36%

commit v1 on v0

--- a/solution.py
+++ b/solution.py
@@ -2,7 +2,6 @@
 
 import jax
 import jax.numpy as jnp
-import numpy as np
 from jax import lax
 from jax.experimental import pallas as pl
 from jax.experimental.pallas import tpu as pltpu
@@ -12,7 +11,6 @@
 LANES = 128
 CHUNK = 16
 STAGE = 4
-VMEM_LIMIT = 56 * 2**20
 HBM = pl.BlockSpec(memory_space=pl.ANY)
 VMEM = pl.BlockSpec(memory_space=pltpu.VMEM)
 
@@ -65,6 +63,23 @@
             stacked[pl.ds(at[2], CHUNK), place] = low
 
 
+def fill_spread(plan, odd, spread):
+    row = lax.broadcasted_iota(jnp.int32, (48, LANES), 0)
+    lane = lax.broadcasted_iota(jnp.int32, (48, LANES), 1)
+    part, item = row // 16, row % 16
+    for a in range(3):
+        for b in range(3):
+            hit = item == jnp.where(odd, 3 * a + b, 3 * (2 - a) + b)
+            if b == 0:
+                hit = jnp.logical_and(hit, lane != LANES - 1)
+            if b == 2:
+                hit = jnp.logical_and(hit, lane != 0)
+            at = LANES * (3 * a + b)
+            spread[:, at : at + LANES] = jnp.where(hit, 1.0, 0.0).astype(BF16)
+    hit = jnp.logical_and(item == 9, lane == plan.bias_lane + part)
+    spread[:, 9 * LANES :] = jnp.where(hit, 1.0, 0.0).astype(BF16)
+
+
 def make_taps(kern, spread, taps):
     high = kern.astype(BF16)
     rest = kern - high.astype(F32)
@@ -122,7 +137,7 @@
         functools.partial(edges_kernel, plan),
         out_shape=[shape, shape],
         in_specs=[HBM],
-        out_specs=[HBM, HBM],
+        out_specs=[VMEM, VMEM],
         scratch_shapes=[pltpu.SemaphoreType.DMA((2,))],
     )(source)
 
@@ -139,14 +154,16 @@
     own, side = plan.own, STAGE
     refs = list(refs)
     inputs = [refs.pop(0) for _ in range(2 if first else 4)]
-    weights, kern, spread = refs.pop(0), refs.pop(0), refs.pop(0)
+    weights, kern_in = refs.pop(0), refs.pop(0)
     mixes = refs.pop(0)
     behind = [refs.pop(0) for _ in range(STAGE)]
     final = refs.pop(0)
     sums = None if first else refs.pop(0)
     rows = [refs.pop(0) for _ in range(STAGE + 1)]
-    weight, mix, taps, stacked, sem_rows, sem_w, sem_out = refs
+    kern, spread, weight, mix, taps, stacked, sem_k, sem_rows, sem_w, sem_out = refs
     odd, _ = plan.position()
+    taps_in = pltpu.make_async_copy(kern_in.at[pl.ds(start, STAGE)], kern, sem_k.at[0])
+    taps_in.start()
 
     arrive = []
     for l in range(STAGE):
@@ -175,10 +192,11 @@
         move.start()
     for copy in arrive[1:]:
         copy.start()
-    picked = spread[jnp.where(odd, 1, 0)]
-    make_taps(kern[start], picked, taps.at[0])
+    fill_spread(plan, odd, spread)
     for s in range(2):
         fill_ones(plan, stacked.at[s])
+    taps_in.wait()
+    make_taps(kern[0], spread[...], taps.at[0])
     leave = []
 
     def send(index, source, target):
@@ -201,7 +219,7 @@
 
         def between(l=l):
             if l + 1 < STAGE:
-                make_taps(kern[start + l + 1], picked, taps.at[(l + 1) % 2])
+                make_taps(kern[l + 1], spread[...], taps.at[(l + 1) % 2])
                 arrive[l + 1].wait()
                 make_mix(plan, weight.at[l + 1], taps.at[(l + 1) % 2], mix.at[l + 1])
 
@@ -222,7 +240,7 @@
         copy.wait()
 
 
-def trapezoid(plan, start, inputs, weights, kern, spread):
+def trapezoid(plan, start, inputs, weights, kern):
     channels, width = plan.channels, inputs[0].shape[-1]
     first = start == 0
     shape = lambda *s: jax.ShapeDtypeStruct(s, F32)
@@ -237,50 +255,62 @@
     return pl.pallas_call(
         functools.partial(trapezoid_kernel, plan, start),
         out_shape=outs,
-        in_specs=[HBM] * (len(inputs) + 1) + [VMEM, VMEM],
+        in_specs=[HBM] * (len(inputs) + 2),
         out_specs=specs,
         scratch_shapes=[pltpu.VMEM((reach - 2 * l, channels, width), F32) for l in range(STAGE + 1)]
         + [
+            pltpu.VMEM((STAGE, 16, channels), F32),
+            pltpu.VMEM((48, 10 * LANES), BF16),
             pltpu.VMEM((STAGE, channels, channels), F32),
             pltpu.VMEM((STAGE, channels, plan.depth), BF16),
             pltpu.VMEM((2, channels, 10 * LANES), F32),
             pltpu.VMEM((2, plan.depth, LANES * (reach - 2)), BF16),
+            pltpu.SemaphoreType.DMA((1,)),
             pltpu.SemaphoreType.DMA((reach,)),
             pltpu.SemaphoreType.DMA((STAGE,)),
             pltpu.SemaphoreType.DMA((3 * STAGE,)),
         ],
-        compiler_params=pltpu.CompilerParams(vmem_limit_bytes=VMEM_LIMIT),
-    )(*inputs, weights, kern, spread)
-
-
-def wave_kernel(plan, start, stop, count, base, order, keep_from, ending, *refs):
+        compiler_params=pltpu.CompilerParams(vmem_limit_bytes=36 * 2**20),
+    )(*inputs, weights, kern)
+
+
+def wave_kernel(plan, start, stop, pieces, base, keep_from, ending, *refs):
     levels = stop - start
     refs = list(refs)
-    fresh = refs.pop(0)
+    fresh = [refs.pop(0) for _ in pieces]
     behind_in = [refs.pop(0) for _ in range(levels)]
     mixes = [refs.pop(0) for _ in range(2)]
-    kern, spread = refs.pop(0), refs.pop(0)
+    kern_in = refs.pop(0)
     if ending:
         refs.pop(0)
-        sums_in = refs.pop(0)
-    else:
-        sums_in = None
+        sums_in, classes_in = refs.pop(0), refs.pop(0)
     behind_out = {l: refs.pop(0) for l in range(max(start, keep_from), stop)}
+    count = sum(rows for rows, _ in pieces)
     if ending:
-        final, sums = refs.pop(0), refs.pop(0)
+        final, scores = refs.pop(0), refs.pop(0)
     else:
         ends = [refs.pop(0) for _ in range(count // 2)]
     rows = [refs.pop(0) for _ in range(levels + 1)]
-    behind, mix, taps, stacked, sem_rows, sem_b, sem_w, sem_out = refs
+    kern, spread, behind, mix, taps, stacked, sums, classes = refs[:8]
+    sem_k, sem_rows, sem_b, sem_w, sem_out = refs[8:]
     odd, has_next = plan.position()
 
+    taps_in = pltpu.make_async_copy(kern_in.at[pl.ds(start, levels)], kern, sem_k.at[0])
+    taps_in.start()
     moves = []
-    for k in range(count):
-        if order == "mirror":
-            place = jnp.where(odd, k, count - 1 - k)
-        else:
-            place = count - 1 - k
-        moves.append(pltpu.make_async_copy(fresh.at[k], rows[0].at[place], sem_rows.at[k]))
+    at = 0
+    for piece, (size, order) in zip(fresh, pieces):
+        for k in range(size):
+            if order == "mirror":
+                place = jnp.where(odd, k, size - 1 - k)
+            elif order == "reverse":
+                place = size - 1 - k
+            else:
+                place = k
+            moves.append(
+                pltpu.make_async_copy(piece.at[k], rows[0].at[at + place], sem_rows.at[at + k])
+            )
+        at += size
     for move in moves:
         move.start()
     tails, weights = [], []
@@ -290,15 +320,23 @@
         weights.append(
             pltpu.make_async_copy(mixes[block // STAGE].at[block % STAGE], mix.at[l], sem_w.at[l])
         )
-    for l in range(levels):
+    for l in range(min(2, levels)):
         tails[l].start()
         weights[l].start()
-    picked = spread[jnp.where(odd, 1, 0)]
-    make_taps(kern[start], picked, taps.at[0])
+    fill_spread(plan, odd, spread)
     for s in range(2):
         fill_ones(plan, stacked.at[s])
+    taps_in.wait()
+    make_taps(kern[0], spread[...], taps.at[0])
     for move in moves:
         move.wait()
+    if ending:
+        extra = [
+            pltpu.make_async_copy(sums_in, sums, sem_k.at[1]),
+            pltpu.make_async_copy(classes_in, classes, sem_k.at[2]),
+        ]
+        for copy in extra:
+            copy.start()
     leave = []
 
     def send(index, source, target):
@@ -311,6 +349,9 @@
         if start + l in behind_out:
             send(l, source.at[pl.ds(count - 2, 2)], behind_out[start + l])
         tails[l].wait()
+        if l + 2 < levels:
+            tails[l + 2].start()
+            weights[l + 2].start()
 
         def store(k, value, l=l, target=target):
             if base - (start + l + 1) + k >= plan.own:
@@ -319,9 +360,8 @@
 
         def between(l=l):
             if l + 1 < levels:
-                make_taps(kern[start + l + 1], picked, taps.at[(l + 1) % 2])
+                make_taps(kern[l + 1], spread[...], taps.at[(l + 1) % 2])
             weights[l].wait()
-
 
         run_level(
             plan, count // 2,
@@ -336,7 +376,13 @@
         for k in range(count):
             u = base - stop + k
             send(levels + k, last.at[k], final.at[jnp.where(odd, u, plan.own - 1 - u)])
-        add_rows(sums, [sums_in[...]] + [last[k] for k in range(count)])
+        for copy in extra:
+            copy.wait()
+        add_rows(sums, [sums[...]] + [last[k] for k in range(count)])
+        score = jnp.dot(
+            classes[...], sums[...], precision=lax.Precision.HIGHEST, preferred_element_type=F32
+        )
+        scores[...] = jnp.broadcast_to(jnp.sum(score, axis=1, keepdims=True), scores.shape)
     else:
         for p in range(count // 2):
             send(levels + p, last.at[pl.ds(2 * p, 2)], ends[p])
@@ -344,62 +390,52 @@
         copy.wait()
 
 
-def wave(plan, start, stop, base, order, keep_from, fresh, behind, mixes, kern, spread, ending=None):
-    count, channels, width = fresh.shape
+def wave(plan, start, stop, base, keep_from, fresh, orders, behind, mixes, kern, ending=None):
+    channels, width = fresh[0].shape[1:]
+    pieces = tuple((f.shape[0], order) for f, order in zip(fresh, orders))
+    count = sum(rows for rows, _ in pieces)
     levels = stop - start
     pair = jax.ShapeDtypeStruct((2, channels, width), F32)
     outs = [pair] * (stop - max(start, keep_from))
-    operands = [fresh, *behind, *mixes, kern, spread]
-    in_specs = [HBM] * (len(operands) - 2) + [VMEM, VMEM]
+    operands = [*fresh, *behind, *mixes, kern]
     specs = [HBM] * len(outs)
     aliases = {}
     if ending is not None:
         aliases = {len(operands): len(outs)}
         operands += list(ending)
-        in_specs += [HBM, VMEM]
-        outs += [jax.ShapeDtypeStruct(e.shape, F32) for e in ending]
+        outs += [
+            jax.ShapeDtypeStruct(ending[0].shape, F32), jax.ShapeDtypeStruct((8, LANES), F32)
+        ]
         specs += [HBM, VMEM]
     else:
         outs += [pair] * (count // 2)
         specs += [HBM] * (count // 2)
     return pl.pallas_call(
         functools.partial(
-            wave_kernel, plan, start, stop, count, base, order, keep_from, ending is not None
+            wave_kernel, plan, start, stop, pieces, base, keep_from, ending is not None
         ),
         out_shape=outs,
-        in_specs=in_specs,
+        in_specs=[HBM] * len(operands),
         out_specs=specs,
-        scratch_shapes=[pltpu.VMEM(fresh.shape, F32)] * (levels + 1)
+        scratch_shapes=[pltpu.VMEM((count, channels, width), F32)] * (levels + 1)
         + [
+            pltpu.VMEM((levels, 16, channels), F32),
+            pltpu.VMEM((48, 10 * LANES), BF16),
             pltpu.VMEM((levels, 2, channels, width), F32),
             pltpu.VMEM((levels, channels, plan.depth), BF16),
             pltpu.VMEM((2, channels, 10 * LANES), F32),
             pltpu.VMEM((2, plan.depth, LANES * count), BF16),
+            pltpu.VMEM((channels, width), F32),
+            pltpu.VMEM((8, channels), F32),
+            pltpu.SemaphoreType.DMA((3,)),
             pltpu.SemaphoreType.DMA((count,)),
             pltpu.SemaphoreType.DMA((levels,)),
             pltpu.SemaphoreType.DMA((levels,)),
             pltpu.SemaphoreType.DMA((levels + count,)),
         ],
         input_output_aliases=aliases,
-        compiler_params=pltpu.CompilerParams(vmem_limit_bytes=VMEM_LIMIT),
+        compiler_params=pltpu.CompilerParams(vmem_limit_bytes=26 * 2**20),
     )(*operands)
-
-
-def spread_matrix(plan):
-    both = np.zeros((2, 3, 16, 10, LANES), np.float32)
-    for odd in range(2):
-        for part in range(3):
-            for a in range(3):
-                for b in range(3):
-                    row = 3 * (a if odd else 2 - a) + b
-                    line = both[odd, part, row, 3 * a + b]
-                    line[:] = 1.0
-                    if b == 0:
-                        line[LANES - 1] = 0.0
-                    if b == 2:
-                        line[0] = 0.0
-            both[odd, part, 9, 9, plan.bias_lane + part] = 1.0
-    return jnp.asarray(both.reshape(2, 48, 10 * LANES), BF16)
 
 
 def per_device(count, slide_map, kernels, pointwise, biases, classifier):
@@ -414,34 +450,29 @@
     near0, far0 = send(near0, near), send(far0, far)
     kern = jnp.concatenate([kernels.reshape(levels, 9, channels), biases[:, None]], axis=1)
     kern = jnp.pad(kern, ((0, 0), (0, 6), (0, 0)))
-    spread = spread_matrix(plan)
-
-    mix0, t0, t1, t2, t3, low4 = trapezoid(plan, 0, [near0, slide_map], pointwise, kern, spread)
+
+    mix0, t0, t1, t2, t3, low4 = trapezoid(plan, 0, [near0, slide_map], pointwise, kern)
     far2 = send(t2, far)
     near4 = send(low4, near)
     w2, w3, mid4, high4 = wave(
-        plan, 0, 4, own, "mirror", 2, far0, [t0, t1, t2, t3], [mix0, mix0], kern, spread
+        plan, 0, 4, own, 2, [far0], ["mirror"], [t0, t1, t2, t3], [mix0, mix0], kern
     )
     far4 = send(mid4, far)
     mix4, t4, t5, t6, t7, features, sums = trapezoid(
-        plan, 4, [near4, low4, mid4, high4], pointwise, kern, spread
+        plan, 4, [near4, low4, mid4, high4], pointwise, kern
     )
     mixes = [mix0, mix4]
-    w4, w5, w6, w7, features, sums = wave(
-        plan, 2, 8, own + 4, "reverse", 4, far2, [w2, w3, t4, t5, t6, t7], mixes, kern, spread,
-        (features, sums),
+    (next4,) = wave(plan, 2, 4, own + 4, 4, [far2], ["reverse"], [w2, w3], mixes, kern)
+    classes = jnp.pad(classifier.T, ((0, 8 - classifier.shape[1]), (0, 0)))
+    features, part = wave(
+        plan, 4, 8, own + 4, 8, [next4, far4], ["same", "reverse"], [t4, t5, t6, t7], mixes, kern,
+        (features, sums, classes),
     )
-    features, sums = wave(
-        plan, 4, 8, own + 6, "reverse", 8, far4, [w4, w5, w6, w7], mixes, kern, spread,
-        (features, sums),
-    )
-    part = jnp.sum(jnp.sum(sums, axis=1)[:, None] * classifier, axis=0)
-    part = part * (1.0 / (own * count * width))
     stride = 1
     while stride < count:
         part = part + send(part, [(i, i ^ stride) for i in range(count)])
         stride *= 2
-    return features, part
+    return features, part[: classifier.shape[1], 0] * (1.0 / (own * count * width))
 
 
 def solution(mesh):

time: 149 us -> 95.1 us (0.64)
  Pallas kernels: 116 us -> 62.8 us
  waiting for transfers between devices: 8.51 us -> 5.59 us
  local copies, waits for them, and re-layouts: 4.34 us -> 6.15 us
  starting transfers between devices: 17 us -> 18.8 us
  other arithmetic: 2.47 us -> 0.69 us
    pallas_call x1, Pallas kernels: 52.7 us -> 2.63 us  [edges(): pl.pallas_call(functools.partial(edges_kernel, plan), out_shape=[shape, s...]
    pallas_call x3, Pallas kernels: 35.6 us -> 25.1 us  [wave(): pl.pallas_call(functools.partial(wave_kernel, plan, start, stop, pieces,...]
    pallas_call x2, Pallas kernels: 27.6 us -> 35 us  [trapezoid(): pl.pallas_call(functools.partial(trapezoid_kernel, plan, start), out_shap...]
    ppermute x9, waiting for transfers between devices: 8.51 us -> 5.59 us  [per_device(): send = lambda rows, pairs: lax.ppermute(rows, 'space', pairs)]
    ppermute x9, starting transfers between devices: 17 us -> 18.8 us  [per_device(): send = lambda rows, pairs: lax.ppermute(rows, 'space', pairs)]
    unnamed x16 -> x10, local copies, waits for them, and re-layouts: 4.23 us -> 4.41 us
  transfers between devices with their start and end apart: 9 -> 9, of which waited for: 5 -> 4; matrix products, arithmetic and copies ran while one was open for 1% -> 2% of each run, Pallas kernels for 36% -> 53%
where the time goes in v1:
time: 95.1 us; the launch traced here: 94.8 us
  Pallas kernels  62.8 us (66%)
  starting transfers between devices  18.8 us (20%)
  local copies, waits for them, and re-layouts  6.15 us (6%)
  waiting for transfers between devices  5.59 us (6%)
    pallas_call x2, Pallas kernels, trapezoid(): pl.pallas_call(functools.partial(trapezoid_kernel, plan, start), out_shap...  35 us
    pallas_call x3, Pallas kernels, wave(): pl.pallas_call(functools.partial(wave_kernel, plan, start, stop, pieces,...  25.1 us
    ppermute x9, starting transfers between devices, per_device(): send = lambda rows, pairs: lax.ppermute(rows, 'space', pairs)  18.8 us
    ppermute x9, waiting for transfers between devices, per_device(): send = lambda rows, pairs: lax.ppermute(rows, 'space', pairs)  5.59 us
    unnamed x10, local copies, waits for them, and re-layouts  4.41 us
    pallas_call x1, Pallas kernels, edges(): pl.pallas_call(functools.partial(edges_kernel, plan), out_shape=[shape, s...  2.63 us
  transfers between devices with their start and end apart: 9, of which 4 were waited for; matrix products, arithmetic and copies ran while one was open for 2% of the time, Pallas kernels for 53%

profile of v1, /device:TPU:0, one launch (start us, length us, event | category | flops | bytes accessed | tf_op | source)
XLA Modules:
  0.0 94.8 jit_solution(6575657844840999250)
XLA Ops:
  0.6 2.6 %shard_map.68 = (f32[4,416,128]{2,1,0:T(8,128)}, f32[4,416,128]{2,1,0:T(8,128)}) custom-call(f32[8,416,128]{2,1,0:T(8,128)} %refs_1_.1), custom_call_target="tpu_custom_call" | custom-call | tf_op jit(solution)/shard_map/pallas_call | solution.py:136
  3.3 0.5 collective-permute-start
  3.8 0.7 collective-permute-start.2
  4.5 0.7 broadcast_in_dim.3
  5.2 1.0 %copy.9 = f32[8,9,416]{2,1,0:T(8,128)S(1)} copy(f32[8,9,416]{2,0,1:T(8,128)} %bitcast.4) | data formatting | bytes 239616 | tf_op jit(solution)/shard_map/reshape | solution.py:451
  6.3 0.0 collective-permute-done.refs_0_
  6.3 0.0 copy-start
  6.3 2.9 %copy-done = f32[8,416,416]{2,1,0:T(8,128)S(1)} copy-done((f32[8,416,416]{2,1,0:T(8,128)S(1)}, f32[8,416,416]{2,1,0:T(8,128)}, u32[]{:S(2)}) %copy-start) | copy-done | bytes 5537816
  9.3 1.5 %copy-done.1 = f32[8,416,128]{2,1,0:T(8,128)S(1)} copy-done((f32[8,416,128]{2,1,0:T(8,128)S(1)}, f32[8,416,128]{2,1,0:T(8,128)}, u32[]{:S(2)}) %copy-start.1) | copy-done | bytes 1703960
  10.7 17.2 %shard_map.69 = (bf16[4,416,1280]{2,1,0:T(8,128)(2,1)S(1)}, f32[2,416,128]{2,1,0:T(8,128)S(1)}, f32[2,416,128]{2,1,0:T(8,128)S(1)}, f32[2,416,128]{2,1,0:T(8,128...) custom-call(f32[4,416,128]{2,1,0:T(8,128)S(1)} %collective-permute-done.refs_0_, ...), custom_call_target="tpu_custom_call" | custom-call | tf_op jit(solution)/shard_map/pallas_call | solution.py:255
  27.9 3.9 %collective-permute-start.3 = (f32[4,416,128]{2,1,0:T(8,128)S(1)}, f32[4,416,128]{2,1,0:T(8,128)S(1)}, u32[]{:S(2)}, u32[]{:S(2)}) collective-permute-start(f32[4,416,128]{2,1,0:T(8,128)S(1)} %get-tuple-element.32.refs_1_), channel_id=1, source_target_pairs={{0,1},{1,0},{2,3},{3,2},{4,5},{5,4},{6,7},{7,6},{8,9},{9,8},{10,11... | collective-permute-start | bytes 2555912 | tf_op jit(solution)/shard_map/ppermute | solution.py:447
  31.8 0.9 collective-permute-start.1
  32.7 0.0 collective-permute-done.2.refs_0_
  32.7 0.0 copy-start.2
  32.7 0.0 slice-start.1
  32.7 10.1 %shard_map.70 = (f32[2,416,128]{2,1,0:T(8,128)S(1)}, f32[2,416,128]{2,1,0:T(8,128)S(1)}, f32[2,416,128]{2,1,0:T(8,128)S(1)}, f32[2,416,128]{2,1,0:T(8,128)S(1)}) custom-call(f32[4,416,128]{2,1,0:T(8,128)S(1)} %collective-permute-done.2.refs_0_, f32[2,416,128]{2,1,0:T(8,128)S(1)} %get-tuple-element.26.refs_1_, f32[2,416,128]{2,1,0:T(8,128)S(1)} %get-tuple-element.27.refs_2_, ...), custom_call_target="tpu_custom_call" | custom-call | tf_op jit(solution)/shard_map/pallas_call | solution.py:413
  42.8 0.7 collective-permute-start.4
  43.6 0.0 collective-permute-done.3.refs_0_
  43.6 17.8 %shard_map.71 = (bf16[4,416,1280]{2,1,0:T(8,128)(2,1)S(1)}, f32[2,416,128]{2,1,0:T(8,128)S(1)}, f32[2,416,128]{2,1,0:T(8,128)S(1)}, f32[2,416,128]{2,1,0:T(8,128...) custom-call(f32[4,416,128]{2,1,0:T(8,128)S(1)} %collective-permute-done.3.refs_0_, ...), custom_call_target="tpu_custom_call" | custom-call | tf_op jit(solution)/shard_map/pallas_call | solution.py:255
  61.4 0.0 collective-permute-done.1.refs_0_
  61.4 4.7 %shard_map.72.refs_0_ = f32[2,416,128]{2,1,0:T(8,128)S(1)} custom-call(f32[2,416,128]{2,1,0:T(8,128)S(1)} %collective-permute-done.1.refs_0_, f32[2,416,128]{2,1,0:T(8,128)S(1)} %get-tuple-element.30.refs_1_, f32[2,416,128]{2,1,0:T(8,128)S(1)} %get-tuple-element.31.refs_2_, bf16[4,416,1280]{2,1,0:T(8,128)(2,1)S(1)} %get-tuple-element.29.refs_5_.refs_6_.refs_3_, ...), custom_call_target="tpu_custom_call" | custom-call | tf_op jit(solution)/shard_map/pallas_call | solution.py:413
  66.1 0.0 collective-permute-done.4.refs_1_
  66.2 10.3 %shard_map.73 = (f32[8,416,128]{2,1,0:T(8,128)}, f32[8,128]{1,0:T(8,128)S(1)}) custom-call(f32[2,416,128]{2,1,0:T(8,128)S(1)} %shard_map.72.refs_0_, f32[2,416,128]{2,1,0:T(8,128)S(1)} %collective-permute-done.4.refs_1_, f32[2,416,128]{2,1,0:T(8,128)S(1)} %get-tuple-element.36.refs_2_, ...), custom_call_target="tpu_custom_call", output_to_operand_aliasing={{0}: (9, {})} | custom-call | tf_op jit(solution)/shard_map/pallas_call | solution.py:413
  76.5 4.3 %collective-permute-start.5 = (f32[8,128]{1,0:T(8,128)S(1)}, f32[8,128]{1,0:T(8,128)S(1)}, u32[]{:S(2)}, u32[]{:S(2)}) collective-permute-start(f32[8,128]{1,0:T(8,128)S(1)} %get-tuple-element.43), channel_id=1, source_target_pairs={{0,1},{1,0},{2,3},{3,2},{4,5},{5,4},{6,7},{7,6},{8,9},{9,8},{10,11... | collective-permute-start | bytes 12296 | tf_op jit(solution)/shard_map/ppermute | solution.py:447
  80.7 0.8 collective-permute-done.5
  81.6 2.4 %collective-permute-start.6 = (f32[8,128]{1,0:T(8,128)S(1)}, f32[8,128]{1,0:T(8,128)S(1)}, u32[]{:S(2)}, u32[]{:S(2)}) collective-permute-start(f32[8,128]{1,0:T(8,128)S(1)} %add.16), channel_id=1, source_target_pairs={{0,2},{1,3},{2,0},{3,1},{4,6},{5,7},{6,4},{7,5},{8,10},{9,11},{10,... | collective-permute-start | bytes 12296 | tf_op jit(solution)/shard_map/ppermute | solution.py:447
  84.0 1.6 %collective-permute-done.6 = f32[8,128]{1,0:T(8,128)S(1)} collective-permute-done((f32[8,128]{1,0:T(8,128)S(1)}, f32[8,128]{1,0:T(8,128)S(1)}, u32[]{:S(2)}, u32[]{:S(2)}) %collective-permute-start.6) | collective-permute-done | bytes 4128 | tf_op jit(solution)/shard_map/ppermute | solution.py:447
  85.6 2.4 %collective-permute-start.7 = (f32[8,128]{1,0:T(8,128)S(1)}, f32[8,128]{1,0:T(8,128)S(1)}, u32[]{:S(2)}, u32[]{:S(2)}) collective-permute-start(f32[8,128]{1,0:T(8,128)S(1)} %add.17), channel_id=1, source_target_pairs={{0,4},{1,5},{2,6},{3,7},{4,0},{5,1},{6,2},{7,3},{8,12},{9,13},{10,... | collective-permute-start | bytes 12296 | tf_op jit(solution)/shard_map/ppermute | solution.py:447
  88.0 1.6 %collective-permute-done.7 = f32[8,128]{1,0:T(8,128)S(1)} collective-permute-done((f32[8,128]{1,0:T(8,128)S(1)}, f32[8,128]{1,0:T(8,128)S(1)}, u32[]{:S(2)}, u32[]{:S(2)}) %collective-permute-start.7) | collective-permute-done | bytes 4128 | tf_op jit(solution)/shard_map/ppermute | solution.py:447
  89.6 3.0 %collective-permute-start.8 = (f32[8,128]{1,0:T(8,128)S(1)}, f32[8,128]{1,0:T(8,128)S(1)}, u32[]{:S(2)}, u32[]{:S(2)}) collective-permute-start(f32[8,128]{1,0:T(8,128)S(1)} %add.18), channel_id=1, source_target_pairs={{0,8},{1,9},{2,10},{3,11},{4,12},{5,13},{6,14},{7,15},{8,0},{9,1},... | collective-permute-start | bytes 12296 | tf_op jit(solution)/shard_map/ppermute | solution.py:447
  92.6 1.6 %collective-permute-done.8 = f32[8,128]{1,0:T(8,128)S(1)} collective-permute-done((f32[8,128]{1,0:T(8,128)S(1)}, f32[8,128]{1,0:T(8,128)S(1)}, u32[]{:S(2)}, u32[]{:S(2)}) %collective-permute-start.8) | collective-permute-done | bytes 4128 | tf_op jit(solution)/shard_map/ppermute | solution.py:447
  94.2 0.6 multiply_reduce_fusion
  (12 shorter events, 0.1 us)
Async XLA Ops:
  3.3 3.0 %collective-permute-start = (f32[4,416,128]{2,1,0:T(8,128)}, f32[4,416,128]{2,1,0:T(8,128)S(1)}, u32[]{:S(2)}, u32[]{:S(2)}) collective-permute-start(f32[4,416,128]{2,1,0:T(8,128)} %get-tuple-element.23), channel_id=1, source_target_pairs={{0,1},{1,0},{2,3},{3,2},{4,5},{5,4},{6,7},{7,6},{8,9},{9,8},{10,11... | collective-permute-start | bytes 2555912 | tf_op jit(solution)/shard_map/ppermute | solution.py:447
  3.8 28.9 %collective-permute-start.2 = (f32[4,416,128]{2,1,0:T(8,128)}, f32[4,416,128]{2,1,0:T(8,128)S(1)}, u32[]{:S(2)}, u32[]{:S(2)}) collective-permute-start(f32[4,416,128]{2,1,0:T(8,128)} %get-tuple-element.25), channel_id=1, source_target_pairs={{1,2},{3,4},{5,6},{7,8},{9,10},{11,12},{13,14},{2,1},{4,3},{6,5},{... | collective-permute-start | bytes 2555912 | tf_op jit(solution)/shard_map/ppermute | solution.py:447
  6.3 2.9 %copy-start = (f32[8,416,416]{2,1,0:T(8,128)S(1)}, f32[8,416,416]{2,1,0:T(8,128)}, u32[]{:S(2)}) copy-start(f32[8,416,416]{2,1,0:T(8,128)} %refs_4_.1) | copy-start | bytes 16613380
  9.3 1.5 %copy-start.1 = (f32[8,416,128]{2,1,0:T(8,128)S(1)}, f32[8,416,128]{2,1,0:T(8,128)}, u32[]{:S(2)}) copy-start(f32[8,416,128]{2,1,0:T(8,128)} %refs_1_.1) | copy-start | bytes 5111812
  10.7 32.9 %slice-start = ((s8[6815744]{0:T(1024)(128)(4,1)}), s8[4194304]{0:T(1024)(128)(4,1)S(1)}, s32[]{:S(2)}) async-start(s8[6815744]{0:T(1024)(128)(4,1)} %bitcast.2), calls=%async_computation | async-start | bytes 8388608
  27.9 15.6 %collective-permute-start.3 = (f32[4,416,128]{2,1,0:T(8,128)S(1)}, f32[4,416,128]{2,1,0:T(8,128)S(1)}, u32[]{:S(2)}, u32[]{:S(2)}) collective-permute-start(f32[4,416,128]{2,1,0:T(8,128)S(1)} %get-tuple-element.32.refs_1_), channel_id=1, source_target_pairs={{0,1},{1,0},{2,3},{3,2},{4,5},{5,4},{6,7},{7,6},{8,9},{9,8},{10,11... | collective-permute-start | bytes 2555912 | tf_op jit(solution)/shard_map/ppermute | solution.py:447
  31.8 29.6 %collective-permute-start.1 = (f32[2,416,128]{2,1,0:T(8,128)S(1)}, f32[2,416,128]{2,1,0:T(8,128)S(1)}, u32[]{:S(2)}, u32[]{:S(2)}) collective-permute-start(f32[2,416,128]{2,1,0:T(8,128)S(1)} %get-tuple-element.24.refs_3_), channel_id=1, source_target_pairs={{1,2},{3,4},{5,6},{7,8},{9,10},{11,12},{13,14},{2,1},{4,3},{6,5},{... | collective-permute-start | bytes 1277960 | tf_op jit(solution)/shard_map/ppermute | solution.py:447
  32.7 10.8 %copy-start.2 = (f32[416,2]{0,1:T(2,128)S(1)}, f32[416,2]{0,1:T(2,128)}, u32[]{:S(2)}) copy-start(f32[416,2]{0,1:T(2,128)} %param.9) | copy-start | bytes 9988
  32.7 10.9 %slice-start.1 = ((s8[6815744]{0:T(1024)(128)(4,1)}), s8[2621440]{0:T(1024)(128)(4,1)S(1)}, s32[]{:S(2)}) async-start(s8[6815744]{0:T(1024)(128)(4,1)} %bitcast.2), calls=%async_computation.1 | async-start | bytes 5242880
  42.8 23.3 %collective-permute-start.4 = (f32[2,416,128]{2,1,0:T(8,128)S(1)}, f32[2,416,128]{2,1,0:T(8,128)S(1)}, u32[]{:S(2)}, u32[]{:S(2)}) collective-permute-start(f32[2,416,128]{2,1,0:T(8,128)S(1)} %get-tuple-element.33.refs_2_), channel_id=1, source_target_pairs={{1,2},{3,4},{5,6},{7,8},{9,10},{11,12},{13,14},{2,1},{4,3},{6,5},{... | collective-permute-start | bytes 1277960 | tf_op jit(solution)/shard_map/ppermute | solution.py:447
  76.5 5.1 %collective-permute-start.5 = (f32[8,128]{1,0:T(8,128)S(1)}, f32[8,128]{1,0:T(8,128)S(1)}, u32[]{:S(2)}, u32[]{:S(2)}) collective-permute-start(f32[8,128]{1,0:T(8,128)S(1)} %get-tuple-element.43), channel_id=1, source_target_pairs={{0,1},{1,0},{2,3},{3,2},{4,5},{5,4},{6,7},{7,6},{8,9},{9,8},{10,11... | collective-permute-start | bytes 12296 | tf_op jit(solution)/shard_map/ppermute | solution.py:447
  81.6 4.0 %collective-permute-start.6 = (f32[8,128]{1,0:T(8,128)S(1)}, f32[8,128]{1,0:T(8,128)S(1)}, u32[]{:S(2)}, u32[]{:S(2)}) collective-permute-start(f32[8,128]{1,0:T(8,128)S(1)} %add.16), channel_id=1, source_target_pairs={{0,2},{1,3},{2,0},{3,1},{4,6},{5,7},{6,4},{7,5},{8,10},{9,11},{10,... | collective-permute-start | bytes 12296 | tf_op jit(solution)/shard_map/ppermute | solution.py:447
  85.6 4.0 %collective-permute-start.7 = (f32[8,128]{1,0:T(8,128)S(1)}, f32[8,128]{1,0:T(8,128)S(1)}, u32[]{:S(2)}, u32[]{:S(2)}) collective-permute-start(f32[8,128]{1,0:T(8,128)S(1)} %add.17), channel_id=1, source_target_pairs={{0,4},{1,5},{2,6},{3,7},{4,0},{5,1},{6,2},{7,3},{8,12},{9,13},{10,... | collective-permute-start | bytes 12296 | tf_op jit(solution)/shard_map/ppermute | solution.py:447
  89.6 4.6 %collective-permute-start.8 = (f32[8,128]{1,0:T(8,128)S(1)}, f32[8,128]{1,0:T(8,128)S(1)}, u32[]{:S(2)}, u32[]{:S(2)}) collective-permute-start(f32[8,128]{1,0:T(8,128)S(1)} %add.18), channel_id=1, source_target_pairs={{0,8},{1,9},{2,10},{3,11},{4,12},{5,13},{6,14},{7,15},{8,0},{9,1},... | collective-permute-start | bytes 12296 | tf_op jit(solution)/shard_map/ppermute | solution.py:447

commit v2 on v1

--- a/solution.py
+++ b/solution.py
@@ -106,15 +106,19 @@
 
 
 def run_level(plan, pairs, load, old, taps, mix, stacked, store, between=None):
-    for p in range(pairs):
-        depthwise(plan, lambda k, part, p=p: load(2 * p + k, part), taps, stacked, 256 * p)
-    if between is not None:
-        between()
-    for p in range(pairs):
+    def product(p):
         mixed = jnp.dot(mix[...], stacked[:, 256 * p : 256 * (p + 1)], preferred_element_type=F32)
         for r in range(2):
             k = 2 * p + r
             store(k, old(k) + mixed[:, LANES * r : LANES * (r + 1)])
+
+    for p in range(pairs):
+        depthwise(plan, lambda k, part, p=p: load(2 * p + k, part), taps, stacked, 256 * p)
+        if p == 0 and between is not None:
+            between()
+        if p > 0:
+            product(p - 1)
+    product(pairs - 1)
 
 
 def edges_kernel(plan, source, near, far, sems):
@@ -270,7 +274,7 @@
             pltpu.SemaphoreType.DMA((STAGE,)),
             pltpu.SemaphoreType.DMA((3 * STAGE,)),
         ],
-        compiler_params=pltpu.CompilerParams(vmem_limit_bytes=36 * 2**20),
+        compiler_params=pltpu.CompilerParams(vmem_limit_bytes=56 * 2**20),
     )(*inputs, weights, kern)
 
 
@@ -434,7 +438,7 @@
             pltpu.SemaphoreType.DMA((levels + count,)),
         ],
         input_output_aliases=aliases,
-        compiler_params=pltpu.CompilerParams(vmem_limit_bytes=26 * 2**20),
+        compiler_params=pltpu.CompilerParams(vmem_limit_bytes=56 * 2**20),
     )(*operands)
 
 

time: 95.1 us -> 87.7 us (0.922)
  Pallas kernels: 62.8 us -> 52.9 us
  waiting for transfers between devices: 5.59 us -> 7.52 us
  other arithmetic: 0.69 us -> 2.06 us
  starting transfers between devices: 18.8 us -> 17.5 us
    pallas_call x2, Pallas kernels: 35 us -> 26.2 us  [trapezoid(): pl.pallas_call(functools.partial(trapezoid_kernel, plan, start), out_shap...]
    ppermute x9, waiting for transfers between devices: 5.59 us -> 7.52 us  [per_device(): send = lambda rows, pairs: lax.ppermute(rows, 'space', pairs)]
    ppermute x9, starting transfers between devices: 18.8 us -> 17.5 us  [per_device(): send = lambda rows, pairs: lax.ppermute(rows, 'space', pairs)]
    pallas_call x3, Pallas kernels: 25.1 us -> 24 us  [wave(): pl.pallas_call(functools.partial(wave_kernel, plan, start, stop, pieces,...]
    unnamed x10 -> x12, local copies, waits for them, and re-layouts: 4.41 us -> 4.29 us
  transfers between devices with their start and end apart: 9 -> 9, of which waited for: 4 -> 4; matrix products, arithmetic and copies ran while one was open for 2% -> 4% of each run, Pallas kernels for 53% -> 46%
where the time goes in v2:
time: 87.7 us; the launch traced here: 87.4 us
  Pallas kernels  52.9 us (60%)
  starting transfers between devices  17.5 us (20%)
  waiting for transfers between devices  7.52 us (9%)
  local copies, waits for them, and re-layouts  6.63 us (8%)
  other arithmetic  2.06 us (2%)
    pallas_call x2, Pallas kernels, trapezoid(): pl.pallas_call(functools.partial(trapezoid_kernel, plan, start), out_shap...  26.2 us
    pallas_call x3, Pallas kernels, wave(): pl.pallas_call(functools.partial(wave_kernel, plan, start, stop, pieces,...  24 us
    ppermute x9, starting transfers between devices, per_device(): send = lambda rows, pairs: lax.ppermute(rows, 'space', pairs)  17.5 us
    ppermute x9, waiting for transfers between devices, per_device(): send = lambda rows, pairs: lax.ppermute(rows, 'space', pairs)  7.52 us
    unnamed x12, local copies, waits for them, and re-layouts  4.29 us
    pallas_call x1, Pallas kernels, edges(): pl.pallas_call(functools.partial(edges_kernel, plan), out_shape=[shape, s...  2.62 us
  transfers between devices with their start and end apart: 9, of which 4 were waited for; matrix products, arithmetic and copies ran while one was open for 4% of the time, Pallas kernels for 46%

profile of v2, /device:TPU:0, one launch (start us, length us, event | category | flops | bytes accessed | tf_op | source)
XLA Modules:
  0.0 87.4 jit_solution(13770339913005281934)
XLA Ops:
  0.6 2.6 %shard_map.68 = (f32[4,416,128]{2,1,0:T(8,128)}, f32[4,416,128]{2,1,0:T(8,128)}) custom-call(f32[8,416,128]{2,1,0:T(8,128)} %refs_1_.1), custom_call_target="tpu_custom_call" | custom-call | tf_op jit(solution)/shard_map/pallas_call | solution.py:140
  3.3 0.5 collective-permute-start
  3.8 0.7 collective-permute-start.2
  4.5 0.7 broadcast_in_dim.3
  5.2 1.0 %copy.9 = f32[8,9,416]{2,1,0:T(8,128)S(1)} copy(f32[8,9,416]{2,0,1:T(8,128)} %bitcast.2) | data formatting | bytes 239616 | tf_op jit(solution)/shard_map/reshape | solution.py:455
  6.2 0.7 select_maximum_fusion.refs_3_.refs_7_.refs_5_.refs_8_
  7.0 0.0 collective-permute-done.refs_0_
  7.0 0.9 %copy-done.1 = f32[4,416,128]{2,1,0:T(8,128)} copy-done((f32[4,416,128]{2,1,0:T(8,128)}, f32[4,416,128]{2,1,0:T(8,128)S(1)}, u32[]{:S(2)}) %copy-start.1) | copy-done | bytes 851992
  7.9 12.8 %shard_map.69 = (bf16[4,416,1280]{2,1,0:T(8,128)(2,1)}, f32[2,416,128]{2,1,0:T(8,128)}, f32[2,416,128]{2,1,0:T(8,128)}, f32[2,416,128]{2,1,0:T(8,128)}, f32[2,416,128]{2,1,0:T(8,128)}, /*index=5*/f32[4,416,128]{2,1,0:T(8,128)}) custom-call(f32[4,416,128]{2,1,0:T(8,128)} %copy-done.1, f32[8,416,128]{2,1,0:T(8,128)} %refs_1_.1, f32[8,416,416]{2,1,0:T(8,128)} %refs_4_.1, ...), custom_call_target="tpu_custom_call" | custom-call | tf_op jit(solution)/shard_map/pallas_call | solution.py:259
  20.7 3.9 %collective-permute-start.3 = (f32[4,416,128]{2,1,0:T(8,128)}, f32[4,416,128]{2,1,0:T(8,128)S(1)}, u32[]{:S(2)}, u32[]{:S(2)}) collective-permute-start(f32[4,416,128]{2,1,0:T(8,128)} %get-tuple-element.32.refs_1_), channel_id=1, source_target_pairs={{0,1},{1,0},{2,3},{3,2},{4,5},{5,4},{6,7},{7,6},{8,9},{9,8},{10,11... | collective-permute-start | bytes 2555912 | tf_op jit(solution)/shard_map/ppermute | solution.py:451
  24.6 0.9 collective-permute-start.1
  25.5 0.0 copy-start.2
  25.5 0.9 %copy-done.2 = f32[4,416,128]{2,1,0:T(8,128)} copy-done((f32[4,416,128]{2,1,0:T(8,128)}, f32[4,416,128]{2,1,0:T(8,128)S(1)}, u32[]{:S(2)}) %copy-start.2) | copy-done | bytes 851992
  26.4 8.9 %shard_map.70 = (f32[2,416,128]{2,1,0:T(8,128)}, f32[2,416,128]{2,1,0:T(8,128)}, f32[2,416,128]{2,1,0:T(8,128)}, f32[2,416,128]{2,1,0:T(8,128)}) custom-call(f32[4,416,128]{2,1,0:T(8,128)} %copy-done.2, f32[2,416,128]{2,1,0:T(8,128)} %get-tuple-element.26.refs_1_, f32[2,416,128]{2,1,0:T(8,128)} %get-tuple-element.27.refs_2_, ...), custom_call_target="tpu_custom_call" | custom-call | tf_op jit(solution)/shard_map/pallas_call | solution.py:417
  35.3 0.7 collective-permute-start.4
  36.0 0.6 pad.9.refs_11_
  36.6 0.9 %copy-done = f32[4,416,128]{2,1,0:T(8,128)} copy-done((f32[4,416,128]{2,1,0:T(8,128)}, f32[4,416,128]{2,1,0:T(8,128)S(1)}, u32[]{:S(2)}) %copy-start) | copy-done | bytes 851992
  37.5 13.5 %shard_map.71 = (bf16[4,416,1280]{2,1,0:T(8,128)(2,1)}, f32[2,416,128]{2,1,0:T(8,128)}, f32[2,416,128]{2,1,0:T(8,128)}, f32[2,416,128]{2,1,0:T(8,128)}, f32[2,41...) custom-call(f32[4,416,128]{2,1,0:T(8,128)} %copy-done, f32[4,416,128]{2,1,0:T(8,128)} %get-tuple-element.32.refs_1_, ...), custom_call_target="tpu_custom_call" | custom-call | tf_op jit(solution)/shard_map/pallas_call | solution.py:259
  51.0 0.8 copy-done.3
  51.8 5.1 %shard_map.72.refs_0_ = f32[2,416,128]{2,1,0:T(8,128)} custom-call(f32[2,416,128]{2,1,0:T(8,128)} %copy-done.3, f32[2,416,128]{2,1,0:T(8,128)} %get-tuple-element.30.refs_1_, f32[2,416,128]{2,1,0:T(8,128)} %get-tuple-element.31.refs_2_, bf16[4,416,1280]{2,1,0:T(8,128)(2,1)} %get-tuple-element.29.refs_5_.refs_6_.refs_3_, ...), custom_call_target="tpu_custom_call" | custom-call | tf_op jit(solution)/shard_map/pallas_call | solution.py:417
  57.0 0.8 copy-done.4
  57.8 9.9 %shard_map.73 = (f32[8,416,128]{2,1,0:T(8,128)}, f32[8,128]{1,0:T(8,128)}) custom-call(f32[2,416,128]{2,1,0:T(8,128)} %shard_map.72.refs_0_, f32[2,416,128]{2,1,0:T(8,128)} %copy-done.4, f32[2,416,128]{2,1,0:T(8,128)} %get-tuple-element.36.refs_2_, f32[2,416,128]{2,1,0:T(8,128)} %get-tuple-element.37.refs_3_, ...), custom_call_target="tpu_custom_call", output_to_operand_aliasing={{0}: (9, {})} | custom-call | tf_op jit(solution)/shard_map/pallas_call | solution.py:417
  67.7 5.6 %collective-permute-start.5 = (f32[8,128]{1,0:T(8,128)}, f32[8,128]{1,0:T(8,128)S(1)}, u32[]{:S(2)}, u32[]{:S(2)}) collective-permute-start(f32[8,128]{1,0:T(8,128)} %get-tuple-element.43), channel_id=1, source_target_pairs={{0,1},{1,0},{2,3},{3,2},{4,5},{5,4},{6,7},{7,6},{8,9},{9,8},{10,11... | collective-permute-start | bytes 12296 | tf_op jit(solution)/shard_map/ppermute | solution.py:451
  73.3 1.0 %collective-permute-done.5 = f32[8,128]{1,0:T(8,128)S(1)} collective-permute-done((f32[8,128]{1,0:T(8,128)}, f32[8,128]{1,0:T(8,128)S(1)}, u32[]{:S(2)}, u32[]{:S(2)}) %collective-permute-start.5) | collective-permute-done | bytes 4128 | tf_op jit(solution)/shard_map/ppermute | solution.py:451
  74.4 0.7 add.16
  75.0 1.1 %collective-permute-start.6 = (f32[8,128]{1,0:T(8,128)S(1)}, f32[8,128]{1,0:T(8,128)S(1)}, u32[]{:S(2)}, u32[]{:S(2)}) collective-permute-start(f32[8,128]{1,0:T(8,128)S(1)} %add.16), channel_id=1, source_target_pairs={{0,2},{1,3},{2,0},{3,1},{4,6},{5,7},{6,4},{7,5},{8,10},{9,11},{10,... | collective-permute-start | bytes 12296 | tf_op jit(solution)/shard_map/ppermute | solution.py:451
  76.1 2.5 %collective-permute-done.6 = f32[8,128]{1,0:T(8,128)S(1)} collective-permute-done((f32[8,128]{1,0:T(8,128)S(1)}, f32[8,128]{1,0:T(8,128)S(1)}, u32[]{:S(2)}, u32[]{:S(2)}) %collective-permute-start.6) | collective-permute-done | bytes 4128 | tf_op jit(solution)/shard_map/ppermute | solution.py:451
  78.7 1.6 %collective-permute-start.7 = (f32[8,128]{1,0:T(8,128)S(1)}, f32[8,128]{1,0:T(8,128)S(1)}, u32[]{:S(2)}, u32[]{:S(2)}) collective-permute-start(f32[8,128]{1,0:T(8,128)S(1)} %add.17), channel_id=1, source_target_pairs={{0,4},{1,5},{2,6},{3,7},{4,0},{5,1},{6,2},{7,3},{8,12},{9,13},{10,... | collective-permute-start | bytes 12296 | tf_op jit(solution)/shard_map/ppermute | solution.py:451
  80.2 2.0 %collective-permute-done.7 = f32[8,128]{1,0:T(8,128)S(1)} collective-permute-done((f32[8,128]{1,0:T(8,128)S(1)}, f32[8,128]{1,0:T(8,128)S(1)}, u32[]{:S(2)}, u32[]{:S(2)}) %collective-permute-start.7) | collective-permute-done | bytes 4128 | tf_op jit(solution)/shard_map/ppermute | solution.py:451
  82.3 2.6 %collective-permute-start.8 = (f32[8,128]{1,0:T(8,128)S(1)}, f32[8,128]{1,0:T(8,128)S(1)}, u32[]{:S(2)}, u32[]{:S(2)}) collective-permute-start(f32[8,128]{1,0:T(8,128)S(1)} %add.18), channel_id=1, source_target_pairs={{0,8},{1,9},{2,10},{3,11},{4,12},{5,13},{6,14},{7,15},{8,0},{9,1},... | collective-permute-start | bytes 12296 | tf_op jit(solution)/shard_map/ppermute | solution.py:451
  84.8 1.9 %collective-permute-done.8 = f32[8,128]{1,0:T(8,128)S(1)} collective-permute-done((f32[8,128]{1,0:T(8,128)S(1)}, f32[8,128]{1,0:T(8,128)S(1)}, u32[]{:S(2)}, u32[]{:S(2)}) %collective-permute-start.8) | collective-permute-done | bytes 4128 | tf_op jit(solution)/shard_map/ppermute | solution.py:451
  86.8 0.6 multiply_reduce_fusion
  (13 shorter events, 0.0 us)
Async XLA Ops:
  3.3 3.7 %collective-permute-start = (f32[4,416,128]{2,1,0:T(8,128)}, f32[4,416,128]{2,1,0:T(8,128)S(1)}, u32[]{:S(2)}, u32[]{:S(2)}) collective-permute-start(f32[4,416,128]{2,1,0:T(8,128)} %get-tuple-element.23), channel_id=1, source_target_pairs={{0,1},{1,0},{2,3},{3,2},{4,5},{5,4},{6,7},{7,6},{8,9},{9,8},{10,11... | collective-permute-start | bytes 2555912 | tf_op jit(solution)/shard_map/ppermute | solution.py:451
  3.8 21.7 %collective-permute-start.2 = (f32[4,416,128]{2,1,0:T(8,128)}, f32[4,416,128]{2,1,0:T(8,128)S(1)}, u32[]{:S(2)}, u32[]{:S(2)}) collective-permute-start(f32[4,416,128]{2,1,0:T(8,128)} %get-tuple-element.25), channel_id=1, source_target_pairs={{1,2},{3,4},{5,6},{7,8},{9,10},{11,12},{13,14},{2,1},{4,3},{6,5},{... | collective-permute-start | bytes 2555912 | tf_op jit(solution)/shard_map/ppermute | solution.py:451
  7.0 0.9 %copy-start.1 = (f32[4,416,128]{2,1,0:T(8,128)}, f32[4,416,128]{2,1,0:T(8,128)S(1)}, u32[]{:S(2)}) copy-start(f32[4,416,128]{2,1,0:T(8,128)S(1)} %collective-permute-done.refs_0_) | copy-start | bytes 2555908
  20.7 16.0 %collective-permute-start.3 = (f32[4,416,128]{2,1,0:T(8,128)}, f32[4,416,128]{2,1,0:T(8,128)S(1)}, u32[]{:S(2)}, u32[]{:S(2)}) collective-permute-start(f32[4,416,128]{2,1,0:T(8,128)} %get-tuple-element.32.refs_1_), channel_id=1, source_target_pairs={{0,1},{1,0},{2,3},{3,2},{4,5},{5,4},{6,7},{7,6},{8,9},{9,8},{10,11... | collective-permute-start | bytes 2555912 | tf_op jit(solution)/shard_map/ppermute | solution.py:451
  24.6 26.4 %collective-permute-start.1 = (f32[2,416,128]{2,1,0:T(8,128)}, f32[2,416,128]{2,1,0:T(8,128)S(1)}, u32[]{:S(2)}, u32[]{:S(2)}) collective-permute-start(f32[2,416,128]{2,1,0:T(8,128)} %get-tuple-element.24.refs_3_), channel_id=1, source_target_pairs={{1,2},{3,4},{5,6},{7,8},{9,10},{11,12},{13,14},{2,1},{4,3},{6,5},{... | collective-permute-start | bytes 1277960 | tf_op jit(solution)/shard_map/ppermute | solution.py:451
  25.5 0.9 %copy-start.2 = (f32[4,416,128]{2,1,0:T(8,128)}, f32[4,416,128]{2,1,0:T(8,128)S(1)}, u32[]{:S(2)}) copy-start(f32[4,416,128]{2,1,0:T(8,128)S(1)} %collective-permute-done.2.refs_0_) | copy-start | bytes 2555908
  26.4 9.7 %copy-start.5 = (f32[416,2]{0,1:T(2,128)S(1)}, f32[416,2]{0,1:T(2,128)}, u32[]{:S(2)}) copy-start(f32[416,2]{0,1:T(2,128)} %param.9) | copy-start | bytes 9988
  35.3 21.7 %collective-permute-start.4 = (f32[2,416,128]{2,1,0:T(8,128)}, f32[2,416,128]{2,1,0:T(8,128)S(1)}, u32[]{:S(2)}, u32[]{:S(2)}) collective-permute-start(f32[2,416,128]{2,1,0:T(8,128)} %get-tuple-element.33.refs_2_), channel_id=1, source_target_pairs={{1,2},{3,4},{5,6},{7,8},{9,10},{11,12},{13,14},{2,1},{4,3},{6,5},{... | collective-permute-start | bytes 1277960 | tf_op jit(solution)/shard_map/ppermute | solution.py:451
  36.6 0.9 %copy-start = (f32[4,416,128]{2,1,0:T(8,128)}, f32[4,416,128]{2,1,0:T(8,128)S(1)}, u32[]{:S(2)}) copy-start(f32[4,416,128]{2,1,0:T(8,128)S(1)} %collective-permute-done.3.refs_0_) | copy-start | bytes 2555908
  51.0 0.8 copy-start.3
  57.0 0.8 copy-start.4
  67.7 6.6 %collective-permute-start.5 = (f32[8,128]{1,0:T(8,128)}, f32[8,128]{1,0:T(8,128)S(1)}, u32[]{:S(2)}, u32[]{:S(2)}) collective-permute-start(f32[8,128]{1,0:T(8,128)} %get-tuple-element.43), channel_id=1, source_target_pairs={{0,1},{1,0},{2,3},{3,2},{4,5},{5,4},{6,7},{7,6},{8,9},{9,8},{10,11... | collective-permute-start | bytes 12296 | tf_op jit(solution)/shard_map/ppermute | solution.py:451
  75.0 3.6 %collective-permute-start.6 = (f32[8,128]{1,0:T(8,128)S(1)}, f32[8,128]{1,0:T(8,128)S(1)}, u32[]{:S(2)}, u32[]{:S(2)}) collective-permute-start(f32[8,128]{1,0:T(8,128)S(1)} %add.16), channel_id=1, source_target_pairs={{0,2},{1,3},{2,0},{3,1},{4,6},{5,7},{6,4},{7,5},{8,10},{9,11},{10,... | collective-permute-start | bytes 12296 | tf_op jit(solution)/shard_map/ppermute | solution.py:451
  78.7 3.6 %collective-permute-start.7 = (f32[8,128]{1,0:T(8,128)S(1)}, f32[8,128]{1,0:T(8,128)S(1)}, u32[]{:S(2)}, u32[]{:S(2)}) collective-permute-start(f32[8,128]{1,0:T(8,128)S(1)} %add.17), channel_id=1, source_target_pairs={{0,4},{1,5},{2,6},{3,7},{4,0},{5,1},{6,2},{7,3},{8,12},{9,13},{10,... | collective-permute-start | bytes 12296 | tf_op jit(solution)/shard_map/ppermute | solution.py:451
  82.3 4.5 %collective-permute-start.8 = (f32[8,128]{1,0:T(8,128)S(1)}, f32[8,128]{1,0:T(8,128)S(1)}, u32[]{:S(2)}, u32[]{:S(2)}) collective-permute-start(f32[8,128]{1,0:T(8,128)S(1)} %add.18), channel_id=1, source_target_pairs={{0,8},{1,9},{2,10},{3,11},{4,12},{5,13},{6,14},{7,15},{8,0},{9,1},... | collective-permute-start | bytes 12296 | tf_op jit(solution)/shard_map/ppermute | solution.py:451

commit v3 on v2

--- a/solution.py
+++ b/solution.py
@@ -289,7 +289,8 @@
         refs.pop(0)
         sums_in, classes_in = refs.pop(0), refs.pop(0)
     behind_out = {l: refs.pop(0) for l in range(max(start, keep_from), stop)}
-    count = sum(rows for rows, _ in pieces)
+    counts = row_counts(pieces, levels)
+    count = counts[levels]
     if ending:
         final, scores = refs.pop(0), refs.pop(0)
     else:
@@ -303,20 +304,19 @@
     taps_in.start()
     moves = []
     at = 0
-    for piece, (size, order) in zip(fresh, pieces):
+    for piece, (size, order, join) in zip(fresh, pieces):
         for k in range(size):
             if order == "mirror":
                 place = jnp.where(odd, k, size - 1 - k)
-            elif order == "reverse":
+            else:
                 place = size - 1 - k
-            else:
-                place = k
             moves.append(
-                pltpu.make_async_copy(piece.at[k], rows[0].at[at + place], sem_rows.at[at + k])
+                (join, pltpu.make_async_copy(piece.at[k], rows[join].at[at + place], sem_rows.at[at + k]))
             )
         at += size
-    for move in moves:
-        move.start()
+    for join, move in moves:
+        if join == 0:
+            move.start()
     tails, weights = [], []
     for l in range(levels):
         tails.append(pltpu.make_async_copy(behind_in[l], behind.at[l], sem_b.at[l]))
@@ -332,8 +332,12 @@
         fill_ones(plan, stacked.at[s])
     taps_in.wait()
     make_taps(kern[0], spread[...], taps.at[0])
-    for move in moves:
-        move.wait()
+    for join, move in moves:
+        if join > 0:
+            move.start()
+    for join, move in moves:
+        if join == 0:
+            move.wait()
     if ending:
         extra = [
             pltpu.make_async_copy(sums_in, sums, sem_k.at[1]),
@@ -350,8 +354,11 @@
 
     for l in range(levels):
         source, target = rows[l], rows[l + 1]
+        for join, move in moves:
+            if join == l and l > 0:
+                move.wait()
         if start + l in behind_out:
-            send(l, source.at[pl.ds(count - 2, 2)], behind_out[start + l])
+            send(l, source.at[pl.ds(counts[l] - 2, 2)], behind_out[start + l])
         tails[l].wait()
         if l + 2 < levels:
             tails[l + 2].start()
@@ -368,7 +375,7 @@
             weights[l].wait()
 
         run_level(
-            plan, count // 2,
+            plan, counts[l] // 2,
             lambda k, part, l=l, source=source: (
                 behind[l, k, part, :] if k < 2 else source[k - 2, part, :]
             ),
@@ -394,11 +401,16 @@
         copy.wait()
 
 
-def wave(plan, start, stop, base, keep_from, fresh, orders, behind, mixes, kern, ending=None):
+def row_counts(pieces, levels):
+    return [sum(size for size, _, join in pieces if join <= l) for l in range(levels + 1)]
+
+
+def wave(plan, start, stop, base, keep_from, fresh, orders, joins, behind, mixes, kern, ending=None):
     channels, width = fresh[0].shape[1:]
-    pieces = tuple((f.shape[0], order) for f, order in zip(fresh, orders))
-    count = sum(rows for rows, _ in pieces)
+    pieces = tuple((f.shape[0], order, join) for f, order, join in zip(fresh, orders, joins))
     levels = stop - start
+    counts = row_counts(pieces, levels)
+    count = counts[levels]
     pair = jax.ShapeDtypeStruct((2, channels, width), F32)
     outs = [pair] * (stop - max(start, keep_from))
     operands = [*fresh, *behind, *mixes, kern]
@@ -421,7 +433,7 @@
         out_shape=outs,
         in_specs=[HBM] * len(operands),
         out_specs=specs,
-        scratch_shapes=[pltpu.VMEM((count, channels, width), F32)] * (levels + 1)
+        scratch_shapes=[pltpu.VMEM((c, channels, width), F32) for c in counts]
         + [
             pltpu.VMEM((levels, 16, channels), F32),
             pltpu.VMEM((48, 10 * LANES), BF16),
@@ -459,17 +471,17 @@
     far2 = send(t2, far)
     near4 = send(low4, near)
     w2, w3, mid4, high4 = wave(
-        plan, 0, 4, own, 2, [far0], ["mirror"], [t0, t1, t2, t3], [mix0, mix0], kern
+        plan, 0, 4, own, 2, [far0], ["mirror"], [0], [t0, t1, t2, t3], [mix0, mix0], kern
     )
     far4 = send(mid4, far)
     mix4, t4, t5, t6, t7, features, sums = trapezoid(
         plan, 4, [near4, low4, mid4, high4], pointwise, kern
     )
     mixes = [mix0, mix4]
-    (next4,) = wave(plan, 2, 4, own + 4, 4, [far2], ["reverse"], [w2, w3], mixes, kern)
     classes = jnp.pad(classifier.T, ((0, 8 - classifier.shape[1]), (0, 0)))
     features, part = wave(
-        plan, 4, 8, own + 4, 8, [next4, far4], ["same", "reverse"], [t4, t5, t6, t7], mixes, kern,
+        plan, 2, 8, own + 4, 8, [far2, far4], ["reverse", "reverse"], [0, 2],
+        [w2, w3, t4, t5, t6, t7], mixes, kern,
         (features, sums, classes),
     )
     stride = 1

time: 87.7 us -> 87 us (level)
  starting transfers between devices: 17.5 us -> 21.4 us
  Pallas kernels: 52.9 us -> 50.7 us
  waiting for transfers between devices: 7.52 us -> 5.8 us
    ppermute x9, starting transfers between devices: 17.5 us -> 21.4 us  [per_device(): send = lambda rows, pairs: lax.ppermute(rows, 'space', pairs)]
    pallas_call x3 -> x2, Pallas kernels: 24 us -> 21.8 us  [wave(): pl.pallas_call(functools.partial(wave_kernel, plan, start, stop, pieces,...]
    ppermute x9, waiting for transfers between devices: 7.52 us -> 5.8 us  [per_device(): send = lambda rows, pairs: lax.ppermute(rows, 'space', pairs)]
    unnamed x12 -> x14, local copies, waits for them, and re-layouts: 4.29 us -> 3.61 us
  transfers between devices with their start and end apart: 9 -> 9, of which waited for: 4 -> 4; matrix products, arithmetic and copies ran while one was open for 4% -> 4% of each run, Pallas kernels for 46% -> 41%
where the time goes in v3:
time: 87 us; the launch traced here: 86.7 us
  Pallas kernels  50.7 us (58%)
  starting transfers between devices  21.4 us (25%)
  local copies, waits for them, and re-layouts  5.95 us (7%)
  waiting for transfers between devices  5.8 us (7%)
  other arithmetic  2.05 us (2%)
    pallas_call x2, Pallas kernels, trapezoid(): pl.pallas_call(functools.partial(trapezoid_kernel, plan, start), out_shap...  26.2 us
    pallas_call x2, Pallas kernels, wave(): pl.pallas_call(functools.partial(wave_kernel, plan, start, stop, pieces,...  21.8 us
    ppermute x9, starting transfers between devices, per_device(): send = lambda rows, pairs: lax.ppermute(rows, 'space', pairs)  21.4 us
    ppermute x9, waiting for transfers between devices, per_device(): send = lambda rows, pairs: lax.ppermute(rows, 'space', pairs)  5.8 us
    unnamed x14, local copies, waits for them, and re-layouts  3.61 us
    pallas_call x1, Pallas kernels, edges(): pl.pallas_call(functools.partial(edges_kernel, plan), out_shape=[shape, s...  2.62 us
  transfers between devices with their start and end apart: 9, of which 4 were waited for; matrix products, arithmetic and copies ran while one was open for 4% of the time, Pallas kernels for 41%

profile of v3, /device:TPU:0, one launch (start us, length us, event | category | flops | bytes accessed | tf_op | source)
XLA Modules:
  0.0 86.7 jit_solution(13138396525440951999)
XLA Ops:
  0.6 2.6 %shard_map.68 = (f32[4,416,128]{2,1,0:T(8,128)}, f32[4,416,128]{2,1,0:T(8,128)}) custom-call(f32[8,416,128]{2,1,0:T(8,128)} %refs_1_.1), custom_call_target="tpu_custom_call" | custom-call | tf_op jit(solution)/shard_map/pallas_call | solution.py:140
  3.3 0.5 collective-permute-start
  3.8 0.7 collective-permute-start.2
  4.5 1.0 %copy.9 = f32[8,9,416]{2,1,0:T(8,128)S(1)} copy(f32[8,9,416]{2,0,1:T(8,128)} %bitcast.2) | data formatting | bytes 239616 | tf_op jit(solution)/shard_map/reshape | solution.py:467
  5.5 0.7 broadcast_in_dim.3
  6.2 0.7 select_maximum_fusion.refs_3_.refs_7_.refs_5_.refs_10_
  7.0 0.0 collective-permute-done.refs_0_
  7.0 0.9 %copy-done.1 = f32[4,416,128]{2,1,0:T(8,128)} copy-done((f32[4,416,128]{2,1,0:T(8,128)}, f32[4,416,128]{2,1,0:T(8,128)S(1)}, u32[]{:S(2)}) %copy-start.1) | copy-done | bytes 851992
  7.9 12.8 %shard_map.69 = (bf16[4,416,1280]{2,1,0:T(8,128)(2,1)}, f32[2,416,128]{2,1,0:T(8,128)}, f32[2,416,128]{2,1,0:T(8,128)}, f32[2,416,128]{2,1,0:T(8,128)}, f32[2,416,128]{2,1,0:T(8,128)}, /*index=5*/f32[4,416,128]{2,1,0:T(8,128)}) custom-call(f32[4,416,128]{2,1,0:T(8,128)} %copy-done.1, f32[8,416,128]{2,1,0:T(8,128)} %refs_1_.1, f32[8,416,416]{2,1,0:T(8,128)} %refs_4_.1, ...), custom_call_target="tpu_custom_call" | custom-call | tf_op jit(solution)/shard_map/pallas_call | solution.py:259
  20.6 3.9 %collective-permute-start.4 = (f32[4,416,128]{2,1,0:T(8,128)}, f32[4,416,128]{2,1,0:T(8,128)S(1)}, u32[]{:S(2)}, u32[]{:S(2)}) collective-permute-start(f32[4,416,128]{2,1,0:T(8,128)} %get-tuple-element.33.refs_1_), channel_id=1, source_target_pairs={{0,1},{1,0},{2,3},{3,2},{4,5},{5,4},{6,7},{7,6},{8,9},{9,8},{10,11... | collective-permute-start | bytes 2555912 | tf_op jit(solution)/shard_map/ppermute | solution.py:463
  24.6 0.9 %copy-done.2 = f32[4,416,128]{2,1,0:T(8,128)} copy-done((f32[4,416,128]{2,1,0:T(8,128)}, f32[4,416,128]{2,1,0:T(8,128)S(1)}, u32[]{:S(2)}) %copy-start.2) | copy-done | bytes 851992
  25.5 9.1 %shard_map.70 = (f32[2,416,128]{2,1,0:T(8,128)}, f32[2,416,128]{2,1,0:T(8,128)}, f32[2,416,128]{2,1,0:T(8,128)}, f32[2,416,128]{2,1,0:T(8,128)}) custom-call(f32[4,416,128]{2,1,0:T(8,128)} %copy-done.2, f32[2,416,128]{2,1,0:T(8,128)} %get-tuple-element.26.refs_1_, f32[2,416,128]{2,1,0:T(8,128)} %get-tuple-element.27.refs_2_, ...), custom_call_target="tpu_custom_call" | custom-call | tf_op jit(solution)/shard_map/pallas_call | solution.py:429
  34.6 0.7 collective-permute-start.3
  35.3 0.7 collective-permute-start.1
  36.0 0.6 pad.9.refs_13_
  36.6 0.0 collective-permute-done.4.refs_0_
  36.6 0.9 %copy-done = f32[4,416,128]{2,1,0:T(8,128)} copy-done((f32[4,416,128]{2,1,0:T(8,128)}, f32[4,416,128]{2,1,0:T(8,128)S(1)}, u32[]{:S(2)}) %copy-start) | copy-done | bytes 851992
  37.5 13.5 %shard_map.71 = (bf16[4,416,1280]{2,1,0:T(8,128)(2,1)}, f32[2,416,128]{2,1,0:T(8,128)}, f32[2,416,128]{2,1,0:T(8,128)}, f32[2,416,128]{2,1,0:T(8,128)}, f32[2,41...) custom-call(f32[4,416,128]{2,1,0:T(8,128)} %copy-done, f32[4,416,128]{2,1,0:T(8,128)} %get-tuple-element.33.refs_1_, ...), custom_call_target="tpu_custom_call" | custom-call | tf_op jit(solution)/shard_map/pallas_call | solution.py:259
  51.0 0.0 collective-permute-done.1.refs_0_
  51.1 0.8 copy-done.3
  51.8 0.1 copy-done.4
  52.0 12.7 %shard_map.72 = (f32[8,416,128]{2,1,0:T(8,128)}, f32[8,128]{1,0:T(8,128)}) custom-call(f32[2,416,128]{2,1,0:T(8,128)} %copy-done.4, f32[2,416,128]{2,1,0:T(8,128)} %copy-done.3, f32[2,416,128]{2,1,0:T(8,128)} %get-tuple-element.31.refs_2_, f32[2,416,128]{2,1,0:T(8,128)} %get-tuple-element.32.refs_3_, ...), custom_call_target="tpu_custom_call", output_to_operand_aliasing={{0}: (11, {})} | custom-call | tf_op jit(solution)/shard_map/pallas_call | solution.py:429
  64.7 7.7 %collective-permute-start.5 = (f32[8,128]{1,0:T(8,128)}, f32[8,128]{1,0:T(8,128)S(1)}, u32[]{:S(2)}, u32[]{:S(2)}) collective-permute-start(f32[8,128]{1,0:T(8,128)} %get-tuple-element.43), channel_id=1, source_target_pairs={{0,1},{1,0},{2,3},{3,2},{4,5},{5,4},{6,7},{7,6},{8,9},{9,8},{10,11... | collective-permute-start | bytes 12296 | tf_op jit(solution)/shard_map/ppermute | solution.py:463
  72.4 1.0 %collective-permute-done.5 = f32[8,128]{1,0:T(8,128)S(1)} collective-permute-done((f32[8,128]{1,0:T(8,128)}, f32[8,128]{1,0:T(8,128)S(1)}, u32[]{:S(2)}, u32[]{:S(2)}) %collective-permute-start.5) | collective-permute-done | bytes 4128 | tf_op jit(solution)/shard_map/ppermute | solution.py:463
  73.4 0.7 add.16
  74.1 2.1 %collective-permute-start.6 = (f32[8,128]{1,0:T(8,128)S(1)}, f32[8,128]{1,0:T(8,128)S(1)}, u32[]{:S(2)}, u32[]{:S(2)}) collective-permute-start(f32[8,128]{1,0:T(8,128)S(1)} %add.16), channel_id=1, source_target_pairs={{0,2},{1,3},{2,0},{3,1},{4,6},{5,7},{6,4},{7,5},{8,10},{9,11},{10,... | collective-permute-start | bytes 12296 | tf_op jit(solution)/shard_map/ppermute | solution.py:463
  76.1 1.6 %collective-permute-done.6 = f32[8,128]{1,0:T(8,128)S(1)} collective-permute-done((f32[8,128]{1,0:T(8,128)S(1)}, f32[8,128]{1,0:T(8,128)S(1)}, u32[]{:S(2)}, u32[]{:S(2)}) %collective-permute-start.6) | collective-permute-done | bytes 4128 | tf_op jit(solution)/shard_map/ppermute | solution.py:463
  77.7 2.1 %collective-permute-start.7 = (f32[8,128]{1,0:T(8,128)S(1)}, f32[8,128]{1,0:T(8,128)S(1)}, u32[]{:S(2)}, u32[]{:S(2)}) collective-permute-start(f32[8,128]{1,0:T(8,128)S(1)} %add.17), channel_id=1, source_target_pairs={{0,4},{1,5},{2,6},{3,7},{4,0},{5,1},{6,2},{7,3},{8,12},{9,13},{10,... | collective-permute-start | bytes 12296 | tf_op jit(solution)/shard_map/ppermute | solution.py:463
  79.9 1.6 %collective-permute-done.7 = f32[8,128]{1,0:T(8,128)S(1)} collective-permute-done((f32[8,128]{1,0:T(8,128)S(1)}, f32[8,128]{1,0:T(8,128)S(1)}, u32[]{:S(2)}, u32[]{:S(2)}) %collective-permute-start.7) | collective-permute-done | bytes 4128 | tf_op jit(solution)/shard_map/ppermute | solution.py:463
  81.4 3.0 %collective-permute-start.8 = (f32[8,128]{1,0:T(8,128)S(1)}, f32[8,128]{1,0:T(8,128)S(1)}, u32[]{:S(2)}, u32[]{:S(2)}) collective-permute-start(f32[8,128]{1,0:T(8,128)S(1)} %add.18), channel_id=1, source_target_pairs={{0,8},{1,9},{2,10},{3,11},{4,12},{5,13},{6,14},{7,15},{8,0},{9,1},... | collective-permute-start | bytes 12296 | tf_op jit(solution)/shard_map/ppermute | solution.py:463
  84.5 1.6 %collective-permute-done.8 = f32[8,128]{1,0:T(8,128)S(1)} collective-permute-done((f32[8,128]{1,0:T(8,128)S(1)}, f32[8,128]{1,0:T(8,128)S(1)}, u32[]{:S(2)}, u32[]{:S(2)}) %collective-permute-start.8) | collective-permute-done | bytes 4128 | tf_op jit(solution)/shard_map/ppermute | solution.py:463
  86.1 0.6 multiply_reduce_fusion
  (14 shorter events, 0.0 us)
Async XLA Ops:
  3.3 3.7 %collective-permute-start = (f32[4,416,128]{2,1,0:T(8,128)}, f32[4,416,128]{2,1,0:T(8,128)S(1)}, u32[]{:S(2)}, u32[]{:S(2)}) collective-permute-start(f32[4,416,128]{2,1,0:T(8,128)} %get-tuple-element.23), channel_id=1, source_target_pairs={{0,1},{1,0},{2,3},{3,2},{4,5},{5,4},{6,7},{7,6},{8,9},{9,8},{10,11... | collective-permute-start | bytes 2555912 | tf_op jit(solution)/shard_map/ppermute | solution.py:463
  3.8 20.8 %collective-permute-start.2 = (f32[4,416,128]{2,1,0:T(8,128)}, f32[4,416,128]{2,1,0:T(8,128)S(1)}, u32[]{:S(2)}, u32[]{:S(2)}) collective-permute-start(f32[4,416,128]{2,1,0:T(8,128)} %get-tuple-element.25), channel_id=1, source_target_pairs={{1,2},{3,4},{5,6},{7,8},{9,10},{11,12},{13,14},{2,1},{4,3},{6,5},{... | collective-permute-start | bytes 2555912 | tf_op jit(solution)/shard_map/ppermute | solution.py:463
  7.0 0.9 %copy-start.1 = (f32[4,416,128]{2,1,0:T(8,128)}, f32[4,416,128]{2,1,0:T(8,128)S(1)}, u32[]{:S(2)}) copy-start(f32[4,416,128]{2,1,0:T(8,128)S(1)} %collective-permute-done.refs_0_) | copy-start | bytes 2555908
  20.6 16.0 %collective-permute-start.4 = (f32[4,416,128]{2,1,0:T(8,128)}, f32[4,416,128]{2,1,0:T(8,128)S(1)}, u32[]{:S(2)}, u32[]{:S(2)}) collective-permute-start(f32[4,416,128]{2,1,0:T(8,128)} %get-tuple-element.33.refs_1_), channel_id=1, source_target_pairs={{0,1},{1,0},{2,3},{3,2},{4,5},{5,4},{6,7},{7,6},{8,9},{9,8},{10,11... | collective-permute-start | bytes 2555912 | tf_op jit(solution)/shard_map/ppermute | solution.py:463
  24.6 0.9 %copy-start.2 = (f32[4,416,128]{2,1,0:T(8,128)}, f32[4,416,128]{2,1,0:T(8,128)S(1)}, u32[]{:S(2)}) copy-start(f32[4,416,128]{2,1,0:T(8,128)S(1)} %collective-permute-done.2.refs_0_) | copy-start | bytes 2555908
  25.5 9.8 %copy-start.5 = (f32[2,416,128]{2,1,0:T(8,128)S(1)}, f32[2,416,128]{2,1,0:T(8,128)}, u32[]{:S(2)}) copy-start(f32[2,416,128]{2,1,0:T(8,128)} %get-tuple-element.24.refs_3_) | copy-start | bytes 1277956
  25.5 10.5 %copy-start.6 = (f32[416,2]{0,1:T(2,128)S(1)}, f32[416,2]{0,1:T(2,128)}, u32[]{:S(2)}) copy-start(f32[416,2]{0,1:T(2,128)} %param.9) | copy-start | bytes 9988
  34.6 16.4 %collective-permute-start.3 = (f32[2,416,128]{2,1,0:T(8,128)}, f32[2,416,128]{2,1,0:T(8,128)S(1)}, u32[]{:S(2)}, u32[]{:S(2)}) collective-permute-start(f32[2,416,128]{2,1,0:T(8,128)} %get-tuple-element.30.refs_2_), channel_id=1, source_target_pairs={{1,2},{3,4},{5,6},{7,8},{9,10},{11,12},{13,14},{2,1},{4,3},{6,5},{... | collective-permute-start | bytes 1277960 | tf_op jit(solution)/shard_map/ppermute | solution.py:463
  35.3 15.7 %collective-permute-start.1 = (f32[2,416,128]{2,1,0:T(8,128)S(1)}, f32[2,416,128]{2,1,0:T(8,128)S(1)}, u32[]{:S(2)}, u32[]{:S(2)}) collective-permute-start(f32[2,416,128]{2,1,0:T(8,128)S(1)} %copy-done.5), channel_id=1, source_target_pairs={{1,2},{3,4},{5,6},{7,8},{9,10},{11,12},{13,14},{2,1},{4,3},{6,5},{... | collective-permute-start | bytes 1277960 | tf_op jit(solution)/shard_map/ppermute | solution.py:463
  36.6 0.9 %copy-start = (f32[4,416,128]{2,1,0:T(8,128)}, f32[4,416,128]{2,1,0:T(8,128)S(1)}, u32[]{:S(2)}) copy-start(f32[4,416,128]{2,1,0:T(8,128)S(1)} %collective-permute-done.4.refs_0_) | copy-start | bytes 2555908
  51.0 0.8 copy-start.3
  51.0 0.9 %copy-start.4 = (f32[2,416,128]{2,1,0:T(8,128)}, f32[2,416,128]{2,1,0:T(8,128)S(1)}, u32[]{:S(2)}) copy-start(f32[2,416,128]{2,1,0:T(8,128)S(1)} %collective-permute-done.1.refs_0_) | copy-start | bytes 1277956
  64.7 8.8 %collective-permute-start.5 = (f32[8,128]{1,0:T(8,128)}, f32[8,128]{1,0:T(8,128)S(1)}, u32[]{:S(2)}, u32[]{:S(2)}) collective-permute-start(f32[8,128]{1,0:T(8,128)} %get-tuple-element.43), channel_id=1, source_target_pairs={{0,1},{1,0},{2,3},{3,2},{4,5},{5,4},{6,7},{7,6},{8,9},{9,8},{10,11... | collective-permute-start | bytes 12296 | tf_op jit(solution)/shard_map/ppermute | solution.py:463
  74.1 3.6 %collective-permute-start.6 = (f32[8,128]{1,0:T(8,128)S(1)}, f32[8,128]{1,0:T(8,128)S(1)}, u32[]{:S(2)}, u32[]{:S(2)}) collective-permute-start(f32[8,128]{1,0:T(8,128)S(1)} %add.16), channel_id=1, source_target_pairs={{0,2},{1,3},{2,0},{3,1},{4,6},{5,7},{6,4},{7,5},{8,10},{9,11},{10,... | collective-permute-start | bytes 12296 | tf_op jit(solution)/shard_map/ppermute | solution.py:463
  77.7 3.7 %collective-permute-start.7 = (f32[8,128]{1,0:T(8,128)S(1)}, f32[8,128]{1,0:T(8,128)S(1)}, u32[]{:S(2)}, u32[]{:S(2)}) collective-permute-start(f32[8,128]{1,0:T(8,128)S(1)} %add.17), channel_id=1, source_target_pairs={{0,4},{1,5},{2,6},{3,7},{4,0},{5,1},{6,2},{7,3},{8,12},{9,13},{10,... | collective-permute-start | bytes 12296 | tf_op jit(solution)/shard_map/ppermute | solution.py:463
  81.4 4.6 %collective-permute-start.8 = (f32[8,128]{1,0:T(8,128)S(1)}, f32[8,128]{1,0:T(8,128)S(1)}, u32[]{:S(2)}, u32[]{:S(2)}) collective-permute-start(f32[8,128]{1,0:T(8,128)S(1)} %add.18), channel_id=1, source_target_pairs={{0,8},{1,9},{2,10},{3,11},{4,12},{5,13},{6,14},{7,15},{8,0},{9,1},... | collective-permute-start | bytes 12296 | tf_op jit(solution)/shard_map/ppermute | solution.py:463
